TPU v7x, 32 devices: a whole 2x2x4 slice. The times are simulated.
32 devices in a mesh: seq: 16 (over z, y, x), head: 2 (over core).
Axes of the slice: x: 2, y: 2, z: 4, core: 2. Of those that a mesh axis runs over, the one named last changes fastest.
Arguments:
- queries: bfloat16 [8192, 1024], P('seq', 'head'), may hold values from -12 to 12
- key_states: bfloat16 [8192, 1024], P('seq', 'head'), may hold values from -5 to 5
- value_states: bfloat16 [8192, 1024], P('seq', 'head'), may hold values from -6 to 6
- out_grad: bfloat16 [8192, 1024], P('seq', 'head'), may hold values from -6 to 6
Outputs:
- normalized: bfloat16 [8192, 1024], P('seq', 'head')
- grad_queries: bfloat16 [8192, 1024], P('seq', 'head')
- grad_keys: bfloat16 [8192, 1024], P('seq', 'head')
- grad_values: bfloat16 [8192, 1024], P('seq', 'head')
All inputs are finite; a program needn't handle non-finite values.
Results may differ from a plain program's by a relative error of at most 0.035.
Values may be sent and summed in bfloat16 or wider, within the bound.
A program may use at most 64 MiB of HBM per device.

v0:
```python
from functools import reduce

import jax
import jax.numpy as jnp
from jax import lax
from jax.sharding import PartitionSpec as P

DH = 128
LEAF = 256
LEVELS = 3


EPSILON = 1e-06


def from_partner(value, axis, distance):
    mask = 2**distance
    pairs = [(source, source ^ mask) for source in range(lax.axis_size(axis))]
    return lax.ppermute(value, axis, pairs)


def halving(source):
    widened = source.astype(jnp.float32)
    paired = widened.reshape(widened.shape[:-2] + (widened.shape[-2] // 2, 2, widened.shape[-1]))
    return ((paired[..., 0, :] + paired[..., 1, :]) * 0.5).astype(jnp.bfloat16)


def query_view(tensor):
    head_count = tensor.shape[0]
    return tensor.reshape(head_count, -1, 2 * LEAF, DH)


def key_view(tensor):
    head_count = tensor.shape[0]
    return tensor.reshape(head_count, -1, 2 * LEAF, DH)


def key_rows(blocks):
    head_count = blocks.shape[0]
    return blocks.reshape(head_count, -1, DH)


def lower_first(my_index, bit_pos):
    return my_index >> bit_pos & 1 == 0


def ordered(mine_first, own_part, other_part, axis_num):
    return jnp.where(
        mine_first,
        jnp.concatenate([own_part, other_part], axis_num),
        jnp.concatenate([other_part, own_part], axis_num),
    )


def attend(query_blocks, key_blocks, value_blocks):
    scores = jnp.einsum(
        "hgqd,hgkd->hgqk", query_blocks, key_blocks, preferred_element_type=jnp.float32
    ) * DH ** (-0.5)
    maxima = scores.max(-1)
    exp_scores = jnp.exp(scores - maxima[..., None])
    rounded = exp_scores.astype(jnp.bfloat16)
    weighted = jnp.einsum(
        "hgqk,hgkd->hgqd", rounded, value_blocks, preferred_element_type=jnp.float32
    )
    return (maxima, exp_scores, rounded, weighted)


def score_grads(exp_scores, grad_blocks, value_blocks, delta_blocks):
    grad_scores = jnp.einsum(
        "hgqd,hgkd->hgqk", grad_blocks, value_blocks, preferred_element_type=jnp.float32
    )
    return (exp_scores * (grad_scores - delta_blocks[..., None])).astype(jnp.bfloat16)


def attend_back(
    query_blocks, key_blocks, value_blocks, exp_scores, rounded, grad_blocks, delta_blocks
):
    grad_logits = score_grads(exp_scores, grad_blocks, value_blocks, delta_blocks)
    grad_query = jnp.einsum(
        "hgqk,hgkd->hgqd", grad_logits, key_blocks, preferred_element_type=jnp.float32
    ) * DH ** (-0.5)
    grad_key = jnp.einsum(
        "hgqk,hgqd->hgkd", grad_logits, query_blocks, preferred_element_type=jnp.float32
    ) * DH ** (-0.5)
    grad_value = jnp.einsum(
        "hgqk,hgqd->hgkd", rounded, grad_blocks, preferred_element_type=jnp.float32
    )
    return (grad_query, grad_key, grad_value)


def owner_grads(partner_query, owned_keys, owned_values, incoming):
    partner_grad, partner_max, partner_delta = incoming
    grad_heads = partner_grad.astype(jnp.bfloat16)
    scores = jnp.einsum(
        "hqd,hkd->hqk", partner_query, owned_keys, preferred_element_type=jnp.float32
    ) * DH ** (-0.5)
    exp_scores = jnp.exp(scores - partner_max[:, :, None])
    rounded = exp_scores.astype(jnp.bfloat16)
    grad_scores = jnp.einsum(
        "hqd,hkd->hqk", grad_heads, owned_values, preferred_element_type=jnp.float32
    )
    grad_logits = (exp_scores * (grad_scores - partner_delta[:, :, None])).astype(jnp.bfloat16)
    grad_key = jnp.einsum(
        "hqk,hqd->hkd", grad_logits, partner_query, preferred_element_type=jnp.float32
    ) * DH ** (-0.5)
    grad_value = jnp.einsum("hqk,hqd->hkd", rounded, grad_heads, preferred_element_type=jnp.float32)
    return (grad_key, grad_value)


def shards(queries, key_states, value_states, out_grad):
    row_count, col_count = queries.shape
    head_count = col_count // DH
    local_levels = (row_count // LEAF).bit_length() - 1
    my_index = lax.axis_index("seq")

    def by_head(tensor):
        return tensor.reshape(row_count, head_count, DH).transpose(1, 0, 2)

    coarse = [jnp.stack([by_head(queries), by_head(key_states), by_head(value_states)])]
    for level_num in range(1, LEVELS):
        coarse.append(halving(coarse[-1]))
    siblings = {}
    for level_num in range(local_levels, LEVELS):
        bit_pos = level_num - local_levels
        gathered = from_partner(coarse[level_num], "seq", bit_pos)
        for lower_bit in range(bit_pos):
            other_rows = from_partner(gathered, "seq", lower_bit)
            gathered = ordered(lower_first(my_index, lower_bit), gathered, other_rows, 2)
        siblings[level_num] = gathered
    stored = {}
    maxima_rows = {}
    maxima_up, sums_up, weighted_up = ([], [], [])
    for level_num in range(LEVELS):
        stretch = 2**level_num
        level_rows = row_count // stretch
        if level_num < local_levels:
            query_blocks = query_view(coarse[level_num][0])
            key_blocks = key_view(coarse[level_num][1])
            value_blocks = key_view(coarse[level_num][2])
        else:
            query_blocks = coarse[level_num][0].reshape(head_count, 1, level_rows, DH)
            key_blocks = siblings[level_num][1].reshape(head_count, 1, LEAF, DH)
            value_blocks = siblings[level_num][2].reshape(head_count, 1, LEAF, DH)
        maxima, exp_scores, rounded, weighted = attend(query_blocks, key_blocks, value_blocks)
        stored[level_num] = (query_blocks, key_blocks, value_blocks, exp_scores, rounded)
        row_maxima = maxima.reshape(head_count, level_rows)
        maxima_rows[level_num] = row_maxima
        maxima_up.append(jnp.repeat(row_maxima, stretch, axis=1))
        sums_up.append(
            jnp.repeat(exp_scores.sum(-1).reshape(head_count, level_rows), stretch, axis=1)
        )
        weighted_up.append(
            jnp.repeat(weighted.reshape(head_count, level_rows, DH), stretch, axis=1)
        )
    highest = reduce(jnp.maximum, maxima_up)
    factors = [
        2.0**level_num * jnp.exp(maxima_up[level_num] - highest) for level_num in range(LEVELS)
    ]
    denominator = factors[0] * sums_up[0]
    numerator = factors[0][..., None] * weighted_up[0]
    for level_num in range(1, LEVELS):
        denominator = denominator + factors[level_num] * sums_up[level_num]
        numerator = numerator + factors[level_num][..., None] * weighted_up[level_num]
    attended = (numerator / denominator[..., None]).astype(jnp.bfloat16)
    attended_wide = attended.astype(jnp.float32)
    full_width = col_count * lax.axis_size("head")
    square_total = lax.psum(jnp.sum(attended_wide * attended_wide, axis=(0, 2)), "head")
    inverse = lax.rsqrt(square_total / full_width + EPSILON)
    normalized = (attended_wide * inverse[None, :, None]).astype(jnp.bfloat16)
    normalized = normalized.transpose(1, 0, 2).reshape(row_count, col_count)
    grad_wide = by_head(out_grad).astype(jnp.float32)
    dot_totals = lax.psum(jnp.sum(grad_wide * attended_wide, axis=(0, 2)), "head")
    grad_attended = (
        inverse[None, :, None] * grad_wide
        - (inverse**3 * dot_totals / full_width)[None, :, None] * attended_wide
    )
    row_dots = jnp.sum(grad_attended * attended_wide, axis=-1)
    level_grads = {}
    for level_num in range(LEVELS):
        stretch = 2**level_num
        level_rows = row_count // stretch
        share_of = factors[level_num] / denominator
        gathered_grad = (
            (share_of[..., None] * grad_attended)
            .reshape(head_count, level_rows, stretch, DH)
            .sum(2)
        )
        delta_rows = (share_of * row_dots).reshape(head_count, level_rows, stretch).sum(2)
        query_blocks, key_blocks, value_blocks, exp_scores, rounded = stored[level_num]
        grad_rounded = gathered_grad.astype(jnp.bfloat16)
        grad_blocks = grad_rounded.reshape(query_blocks.shape)
        delta_blocks = delta_rows.reshape(query_blocks.shape[:3])
        if level_num < local_levels:
            grad_query, grad_key, grad_value = attend_back(
                query_blocks,
                key_blocks,
                value_blocks,
                exp_scores,
                rounded,
                grad_blocks,
                delta_blocks,
            )
            query_part = grad_query.reshape(head_count, level_rows, DH)
            level_grads[level_num] = jnp.stack(
                [query_part, key_rows(grad_key), key_rows(grad_value)]
            )
        else:
            grad_logits = score_grads(exp_scores, grad_blocks, value_blocks, delta_blocks)
            grad_query = jnp.einsum(
                "hgqk,hgkd->hgqd", grad_logits, key_blocks, preferred_element_type=jnp.float32
            ) * DH ** (-0.5)
            query_part = grad_query.reshape(head_count, level_rows, DH)
            bit_pos = level_num - local_levels
            outgoing = (grad_rounded.astype(jnp.float32), maxima_rows[level_num], delta_rows)
            incoming = from_partner((outgoing[0], outgoing[1], outgoing[2]), "seq", bit_pos)
            for lower_bit in range(bit_pos):
                others = from_partner((incoming[0], incoming[1], incoming[2]), "seq", lower_bit)
                mine_first = lower_first(my_index, lower_bit)
                incoming = (
                    ordered(mine_first, incoming[0], others[0], 1),
                    ordered(mine_first, incoming[1], others[1], 1),
                    ordered(mine_first, incoming[2], others[2], 1),
                )
            grad_key, grad_value = owner_grads(
                siblings[level_num][0], coarse[level_num][1], coarse[level_num][2], incoming
            )
            level_grads[level_num] = jnp.stack([query_part, grad_key, grad_value])
    accumulated = level_grads[LEVELS - 1]
    for level_num in reversed(range(LEVELS - 1)):
        accumulated = jnp.repeat(accumulated, 2, axis=2) * 0.5 + level_grads[level_num]
    grads = accumulated.astype(jnp.bfloat16).transpose(0, 2, 1, 3).reshape(3, row_count, col_count)
    return (normalized, grads[0], grads[1], grads[2])


def solution(mesh):
    return jax.shard_map(
        shards,
        mesh=mesh,
        in_specs=(P("seq", "head"), P("seq", "head"), P("seq", "head"), P("seq", "head")),
        out_specs=(P("seq", "head"), P("seq", "head"), P("seq", "head"), P("seq", "head")),
        check_vma=False,
    )
```

profile of v0, /device:TPU:0, one launch (start us, length us, event | category | flops | bytes accessed | tf_op | source)
XLA Modules:
  0.0 138.9 jit_solution(10556295961704040098)
XLA Ops:
  0.7 1.3 copy.192
  4.0 1.5 %fusion.84 = (f32[3,4,128,1,128]{4,3,2,1,0:T(1,128)S(1)}, f32[3,4,128,1,128]{4,3,2,1,0:T(1,128)S(1)}) fusion(bf16[3,4,128,2,128]{4,3,2,1,0:T(2,128)(2,1)S(1)} %bitcast.146), kind=kLoop, calls=%fused_computation.135 | loop fusion | bytes 3145728 | tf_op jit(solution)/shard_map/slice | solution.py:25
  5.6 3.0 %collective-permute-start.1 = (bf16[3,4,128,128]{3,2,1,0:T(8,128)(2,1)S(1)}, bf16[3,4,128,128]{3,2,1,0:T(8,128)(2,1)}, u32[]{:S(2)}, u32[]{:S(2)}) collective-permute-start(bf16[3,4,128,128]{3,2,1,0:T(8,128)(2,1)S(1)} %bitcast.173), channel_id=1, source_target_pairs={{0,4},{2,6},{4,0},{6,2},{8,12},{10,14},{12,8},{14,10},{16,20},{18,... | collective-permute-start | bytes 1179656 | tf_op jit(solution)/shard_map/ppermute | solution.py:19
  9.7 1.5 %collective-permute-start = (bf16[3,4,256,128]{3,2,1,0:T(8,128)(2,1)}, bf16[3,4,256,128]{3,2,1,0:T(8,128)(2,1)}, u32[]{:S(2)}, u32[]{:S(2)}) collective-permute-start(bf16[3,4,256,128]{3,2,1,0:T(8,128)(2,1)} %fusion.99), channel_id=1, source_target_pairs={{0,2},{2,0},{4,6},{6,4},{8,10},{10,8},{12,14},{14,12},{16,18},{18,... | collective-permute-start | bytes 2359304 | tf_op jit(solution)/shard_map/ppermute | solution.py:19
  11.2 6.6 %collective-permute-done.1 = bf16[3,4,128,128]{3,2,1,0:T(8,128)(2,1)} collective-permute-done((bf16[3,4,128,128]{3,2,1,0:T(8,128)(2,1)S(1)}, bf16[3,4,128,128]{3,2,1,0:T(8,128)(2,1)}, u32[]{:S(2)}, u32[]{:S(2)}) %collective-permute-start.1) | collective-permute-done | bytes 393248 | tf_op jit(solution)/shard_map/ppermute | solution.py:19
  17.9 1.7 %collective-permute-start.2 = (bf16[3,4,128,128]{3,2,1,0:T(8,128)(2,1)}, bf16[3,4,128,128]{3,2,1,0:T(8,128)(2,1)}, u32[]{:S(2)}, u32[]{:S(2)}) collective-permute-start(bf16[3,4,128,128]{3,2,1,0:T(8,128)(2,1)} %collective-permute-done.1), channel_id=1, source_target_pairs={{0,2},{2,0},{4,6},{6,4},{8,10},{10,8},{12,14},{14,12},{16,18},{18,... | collective-permute-start | bytes 1179656 | tf_op jit(solution)/shard_map/ppermute | solution.py:19
  19.6 2.7 %multiply_reduce_fusion = (f32[4,512]{1,0:T(4,128)S(1)}, f32[4,512,512]{1,2,0:T(8,128)}) fusion(bf16[4,512,128]{1,2,0:T(8,128)(2,1)S(1)} %bitcast.151, bf16[4,512,128]{1,2,0:T(8,128)(2,1)S(1)} %bitcast.148), kind=kOutput, calls=%fused_computation.2 | convolution fusion | flops 270530560 | bytes 5251072 | tf_op jit(solution)/shard_map/hgqd,hgkd->hgqk/dot_general | solution.py:56
  23.3 2.9 %fusion.1 = f32[4,512]{1,0:T(4,128)S(1)} fusion(f32[4,512,512]{1,2,0:T(8,128)} %get-tuple-element.51, f32[4,512]{1,0:T(4,128)S(1)} %get-tuple-element.50), kind=kLoop, calls=%fused_computation.5 | loop fusion | flops 3143680 | bytes 4210688 | tf_op jit(solution)/shard_map/reduce_sum | solution.py:150
  29.3 1.7 %copy.215 = f32[4,128,4]{1,2,0:T(4,128)} copy(f32[4,128,4]{2,1,0:T(8,128)} %reshape_broadcast_in_dim_reshape.12) | data formatting | bytes 16384 | tf_op jit(solution)/shard_map/reshape;broadcast_in_dim;reshape | solution.py:150
  31.0 1.7 %copy.212 = f32[4,128,4]{1,2,0:T(4,128)} copy(f32[4,128,4]{2,1,0:T(8,128)} %reshape_broadcast_in_dim_reshape.11) | data formatting | bytes 16384 | tf_op jit(solution)/shard_map/reshape;broadcast_in_dim;reshape | solution.py:148
  32.7 1.7 %copy.227 = f32[4,256,2]{1,0,2:T(4,128)} copy(f32[4,256,2]{0,2,1:T(2,128)} %bitcast.178) | data formatting | bytes 16384 | tf_op jit(solution)/shard_map/reshape;broadcast_in_dim;reshape | solution.py:150
  34.3 1.7 %copy.222 = f32[4,256,2]{1,0,2:T(4,128)} copy(f32[4,256,2]{0,2,1:T(2,128)} %bitcast.177) | data formatting | bytes 16384 | tf_op jit(solution)/shard_map/reshape;broadcast_in_dim;reshape | solution.py:148
  36.0 1.5 %collective-permute-done.2 = bf16[3,4,128,128]{3,2,1,0:T(8,128)(2,1)} collective-permute-done((bf16[3,4,128,128]{3,2,1,0:T(8,128)(2,1)}, bf16[3,4,128,128]{3,2,1,0:T(8,128)(2,1)}, u32[]{:S(2)}, u32[]{:S(2)}) %collective-permute-start.2) | collective-permute-done | bytes 393248 | tf_op jit(solution)/shard_map/ppermute | solution.py:19
  37.5 1.6 %maximum_select_fusion = bf16[3,4,256,128]{3,2,1,0:T(8,128)(2,1)S(1)} fusion(bf16[3,4,128,128]{3,2,1,0:T(8,128)(2,1)} %collective-permute-done.2, bf16[3,4,128,128]{3,2,1,0:T(8,128)(2,1)} %collective-permute-done.1, pred[]{:T(512)S(6)} %eq.4), kind=kLoop, calls=%fused_computation.71 | loop fusion | flops 3538944 | bytes 1572865 | tf_op jit(solution)/shard_map/jit(_where)/select_n | solution.py:48
  42.6 1.3 fusion.86
  44.1 1.8 %collective-permute-start.9 = (f32[4,256]{1,0:T(4,128)S(1)}, f32[4,256]{1,0:T(4,128)}, u32[]{:S(2)}, u32[]{:S(2)}) collective-permute-start(f32[4,256]{1,0:T(4,128)S(1)} %get-tuple-element.48), channel_id=1, source_target_pairs={{0,2},{2,0},{4,6},{6,4},{8,10},{10,8},{12,14},{14,12},{16,18},{18,... | collective-permute-start | bytes 12296 | tf_op jit(solution)/shard_map/ppermute | solution.py:19
  47.1 1.5 %broadcast_in_dim.54 = f32[4,128,4]{2,1,0:T(8,128)} broadcast(f32[4,128]{1,0:T(4,128)} %fusion.52), dimensions={0,1} | broadcast | bytes 10240 | tf_op jit(solution)/shard_map/broadcast_in_dim | solution.py:150
  48.6 1.7 %reshape.555 = f32[4,512]{1,0:T(4,128)} reshape(f32[4,128,4]{2,1,0:T(8,128)} %broadcast_in_dim.54) | data formatting | bytes 16384 | tf_op jit(solution)/shard_map/reshape | solution.py:150
  51.0 1.5 %copy.206 = f32[4,256]{0,1:T(8,128)} copy(f32[4,256]{1,0:T(4,128)} %fusion.40) | data formatting | bytes 8192 | tf_op jit(solution)/shard_map/reduce_sum | solution.py:150
  52.5 1.7 %broadcast_in_dim.53 = f32[4,256,2]{0,2,1:T(2,128)} broadcast(f32[4,256]{0,1:T(8,128)} %copy.206), dimensions={0,1} | broadcast | bytes 12288 | tf_op jit(solution)/shard_map/broadcast_in_dim | solution.py:150
  54.2 1.7 %copy.207 = f32[4,512]{1,0:T(4,128)} copy(f32[4,512]{0,1:T(8,128)} %bitcast.161) | data formatting | bytes 16384 | tf_op jit(solution)/shard_map/reshape | solution.py:150
  56.7 1.7 %reshape.549 = f32[4,512]{1,0:T(4,128)} reshape(f32[4,128,4]{2,1,0:T(8,128)} %broadcast_in_dim.50.clone) | data formatting | bytes 16384 | tf_op jit(solution)/shard_map/reshape | solution.py:148
  61.2 1.8 %fusion.42 = f32[4,256,128]{2,1,0:T(8,128)S(1)} fusion(f32[4,256,256]{1,2,0:T(8,128)S(1)} %get-tuple-element.49, f32[4,256]{1,0:T(4,128)S(1)} %get-tuple-element.48, bf16[3,4,256,128]{3,2,1,0:T(8,128)(2,1)} %collective-permute-done), kind=kOutput, calls=%fused_computation.74 | convolution fusion | flops 67633152 | bytes 1839104 | tf_op jit(solution)/shard_map/hgqk,hgkd->hgqd/dot_general | solution.py:62
  64.6 3.3 %fusion.37 = (f32[512]{0:T(512)S(1)}, f32[512]{0:T(512)S(1)}, bf16[4,512,128]{2,1,0:T(8,128)(2,1)}) fusion(f32[512,4,128]{2,0,1:T(8,128)S(1)} %copy.210, f32[4,512]{1,0:T(4,128)S(1)} %get-tuple-element.31, f32[4,512,128]{2,1,0:T(8,128)S(1)} %bitcast.174, f32[4,512]{1,0:T(4,128)S(1)} %get-tuple-element.34, f32[4,512,128]{2,1,0:T(8,128)S(1)} %bitcast.175, ...), kind=kOutput, calls=%fused_computation.63 | convolution fusion | flops 274725888 | bytes 8433664 | tf_op jit(solution)/shard_map/hgqk,hgkd->hgqd/dot_general | solution.py:62
  67.9 2.6 %all-reduce = (f32[512]{0:T(512)S(1)}, f32[512]{0:T(512)S(1)}) all-reduce(f32[512]{0:T(512)S(1)} %get-tuple-element.25, f32[512]{0:T(512)S(1)} %get-tuple-element.24), channel_id=1, replica_groups=mesh['seq'=16,'head'=2] {'head'}, use_global_device_ids=true, to_apply=%region_7.8 | all-reduce | flops 1024 | bytes 8192 | tf_op jit(solution)/shard_map/psum | solution.py:167
  70.5 3.2 %broadcast_multiply_fusion = (f32[4,512,128]{2,1,0:T(8,128)}, f32[4,512,128]{2,1,0:T(8,128)}, f32[4,512]{1,0:T(4,128)S(1)}, bf16[512,4,128]{2,0,1:T(8,128)(2,1)}) fusion(f32[4,512]{1,0:T(4,128)S(1)} %get-tuple-element.30, bf16[4,512,128]{2,1,0:T(8,128)(2,1)} %get-tuple-element.52, f32[512]{0:T(512)S(1)} %get-tuple-element.44, f32[512,4,128]{2,0,1:T(8,128)S(1)} %copy.210, ...), kind=kLoop, calls=%fused_computation.81 | loop fusion | flops 2619392 | bytes 4222976 | tf_op jit(solution)/shard_map/mul | solution.py:184
  76.9 4.8 %convolution_bitcast_fusion = f32[1,4,512,128]{2,3,1,0:T(8,128)} fusion(f32[4,512,512]{1,2,0:T(8,128)} %get-tuple-element.51, f32[4,512]{1,0:T(4,128)S(1)} %get-tuple-element.50, f32[4,512]{1,0:T(4,128)S(1)} %get-tuple-element.29, bf16[4,512,128]{2,1,0:T(8,128)(2,1)} %get-tuple-element.52, f32[512,4,128]{2,0,1:T(8,128)S(1)} %copy.210, ...), kind=kOutput, calls=%fused_computation.19 | convolution fusion | flops 273154048 | bytes 6836224 | tf_op jit(solution)/shard_map/hgqk,hgqd->hgkd/dot_general | solution.py:85
  81.7 1.9 %multiply_convert_fusion = bf16[4,512,512]{1,2,0:T(8,128)(2,1)S(1)} fusion(f32[4,512,512]{1,2,0:T(8,128)S(1)} %copy-done.1, bf16[4,512,128]{1,2,0:T(8,128)(2,1)S(1)} %bitcast.156, f32[4,512]{1,0:T(4,128)S(1)} %get-tuple-element.28, f32[4,512]{1,0:T(4,128)S(1)} %get-tuple-element.50, f32[4,512]{1,0:T(4,128)S(1)} %get-tuple-element.29, ...), kind=kOutput, calls=%fused_computation | convolution fusion | flops 275251200 | bytes 8417280 | tf_op jit(solution)/shard_map/hgqd,hgkd->hgqk/dot_general | solution.py:69
  83.6 1.8 %fusion.12 = f32[1,4,512,128]{2,3,1,0:T(8,128)} fusion(bf16[4,512,512]{1,2,0:T(8,128)(2,1)S(1)} %multiply_convert_fusion, bf16[4,512,128]{1,2,0:T(8,128)(2,1)S(1)} %bitcast.152), kind=kOutput, calls=%fused_computation.31 | convolution fusion | flops 268697600 | bytes 3670016 | tf_op jit(solution)/shard_map/hgqk,hgqd->hgkd/dot_general | solution.py:82
  85.4 1.5 %fusion.11 = f32[1,4,512,128]{2,3,1,0:T(8,128)} fusion(bf16[4,512,128]{1,2,0:T(8,128)(2,1)S(1)} %bitcast.149, bf16[4,512,512]{1,2,0:T(8,128)(2,1)S(1)} %multiply_convert_fusion), kind=kOutput, calls=%fused_computation.29 | convolution fusion | flops 268697600 | bytes 3670016 | tf_op jit(solution)/shard_map/hgqk,hgkd->hgqd/dot_general | solution.py:79
  86.9 1.9 %reduce_sum.107 = bf16[4,128,128]{2,1,0:T(8,128)(2,1)S(1)} reduce(f32[4,128,4,128]{3,2,1,0:T(4,128)} %bitcast.158, f32[]{:T(128)} %constant.21.clone.1), dimensions={2}, to_apply=%region_10.11 | reduce | flops 196608 | bytes 1179652 | tf_op jit(solution)/shard_map/reduce_sum | solution.py:186
  88.8 1.6 %collective-permute-start.5 = (bf16[4,128,128]{2,1,0:T(8,128)(2,1)S(1)}, bf16[4,128,128]{2,1,0:T(8,128)(2,1)}, u32[]{:S(2)}, u32[]{:S(2)}) collective-permute-start(bf16[4,128,128]{2,1,0:T(8,128)(2,1)S(1)} %reduce_sum.107), channel_id=1, source_target_pairs={{0,4},{2,6},{4,0},{6,2},{8,12},{10,14},{12,8},{14,10},{16,20},{18,... | collective-permute-start | bytes 393224 | tf_op jit(solution)/shard_map/ppermute | solution.py:19
  91.7 1.4 %copy.228 = f32[4,128]{0,1:T(8,128)} copy(f32[4,128]{1,0:T(4,128)} %broadcast_multiply_fusion.3) | data formatting | bytes 4096 | tf_op jit(solution)/shard_map/mul | solution.py:162
  93.1 1.4 %multiply_reduce_fusion.2 = f32[4,128]{1,0:T(4,128)} fusion(f32[4,128,4]{1,2,0:T(4,128)S(1)} %copy.218, f32[4,128,4]{1,2,0:T(4,128)S(1)} %copy.217, f32[4,128,4]{1,2,0:T(4,128)S(1)} %copy.213, f32[4,128,4]{1,2,0:T(4,128)S(1)} %copy-done.23, f32[4,128,4]{1,2,0:T(4,128)} %copy.212, f32[4,128]{1,0:T(4,128)} %broadcast_multiply_fusion.3, ...), kind=kLoop, calls=%fused_computation.116 | loop fusion | flops 30208 | bytes 47104 | tf_op jit(solution)/shard_map/reduce_sum | solution.py:188
  95.0 2.5 %reduce_sum.111 = bf16[4,256,128]{2,1,0:T(8,128)(2,1)S(1)} reduce(f32[4,256,2,128]{3,2,1,0:T(2,128)} %bitcast.157, f32[]{:T(128)} %constant.21.clone.1), dimensions={2}, to_apply=%region_13.14 | reduce | flops 131072 | bytes 1310724 | tf_op jit(solution)/shard_map/reduce_sum | solution.py:186
  101.4 2.4 %fusion.24 = f32[1,4,256,128]{3,2,1,0:T(8,128)} fusion(f32[4,256,256]{1,2,0:T(8,128)S(1)} %get-tuple-element.49, f32[4,256]{1,0:T(4,128)S(1)} %multiply_reduce_fusion.1, f32[4,256]{1,0:T(4,128)S(1)} %get-tuple-element.48, bf16[3,4,256,128]{3,2,1,0:T(8,128)(2,1)} %collective-permute-done, bf16[4,256,128]{2,1,0:T(8,128)(2,1)S(1)} %reduce_sum.111), kind=kOutput, calls=%fused_computation.45 | convolution fusion | flops 135397376 | bytes 2367488 | tf_op jit(solution)/shard_map/hgqk,hgkd->hgqd/dot_general | solution.py:209
  103.7 1.7 %collective-permute-start.4 = (f32[4,128]{1,0:T(4,128)}, f32[4,128]{1,0:T(4,128)S(1)}, u32[]{:S(2)}, u32[]{:S(2)}) collective-permute-start(f32[4,128]{1,0:T(4,128)} %collective-permute-done.3), channel_id=1, source_target_pairs={{0,2},{2,0},{4,6},{6,4},{8,10},{10,8},{12,14},{14,12},{16,18},{18,... | collective-permute-start | bytes 6152 | tf_op jit(solution)/shard_map/ppermute | solution.py:19
  105.5 1.4 %fusion.33 = f32[1,4,128,128]{3,2,1,0:T(8,128)S(1)} fusion(f32[4,128,256]{2,1,0:T(8,128)S(1)} %copy-done.5, f32[4,128]{1,0:T(4,128)} %multiply_reduce_fusion.2, f32[4,128]{1,0:T(4,128)S(1)} %get-tuple-element.46, bf16[3,4,256,128]{3,2,1,0:T(8,128)(2,1)} %copy-done.6, bf16[4,128,128]{2,1,0:T(8,128)(2,1)S(1)} %reduce_sum.107), kind=kOutput, calls=%fused_computation.59 | convolution fusion | flops 67698688 | bytes 1445888 | tf_op jit(solution)/shard_map/hgqk,hgkd->hgqd/dot_general | solution.py:209
  109.2 1.7 %collective-permute-start.8 = (f32[4,128]{1,0:T(4,128)}, f32[4,128]{1,0:T(4,128)S(1)}, u32[]{:S(2)}, u32[]{:S(2)}) collective-permute-start(f32[4,128]{1,0:T(4,128)} %collective-permute-done.7), channel_id=1, source_target_pairs={{0,2},{2,0},{4,6},{6,4},{8,10},{10,8},{12,14},{14,12},{16,18},{18,... | collective-permute-start | bytes 6152 | tf_op jit(solution)/shard_map/ppermute | solution.py:19
  111.7 2.4 %collective-permute-done.8 = f32[4,128]{1,0:T(4,128)S(1)} collective-permute-done((f32[4,128]{1,0:T(4,128)}, f32[4,128]{1,0:T(4,128)S(1)}, u32[]{:S(2)}, u32[]{:S(2)}) %collective-permute-start.8) | collective-permute-done | bytes 2080 | tf_op jit(solution)/shard_map/ppermute | solution.py:19
  115.5 1.3 fusion.9
  116.9 3.2 %collective-permute-done.6 = bf16[4,128,128]{2,1,0:T(8,128)(2,1)S(1)} collective-permute-done((bf16[4,128,128]{2,1,0:T(8,128)(2,1)}, bf16[4,128,128]{2,1,0:T(8,128)(2,1)S(1)}, u32[]{:S(2)}, u32[]{:S(2)}) %collective-permute-start.6) | collective-permute-done | bytes 131104 | tf_op jit(solution)/shard_map/ppermute | solution.py:19
  120.1 1.7 %fusion.34 = f32[1,4,128,128]{3,2,1,0:T(8,128)S(1)} fusion(f32[4,256,128]{2,1,0:T(8,128)S(1)} %copy-done.17, f32[4,256]{1,0:T(4,128)S(1)} %maximum_select_fusion.3, f32[4,256]{1,0:T(4,128)S(1)} %maximum_select_fusion.2, bf16[3,4,256,128]{3,2,1,0:T(8,128)(2,1)} %copy-done.6, bf16[3,4,128,1,128]{4,2,1,0,3:T(8,128)(2,1)} %copy-done.14, ...), kind=kOutput, calls=%fused_computation.60 | convolution fusion | flops 68878336 | bytes 1449985 | tf_op jit(solution)/shard_map/hqk,hqd->hkd/dot_general | solution.py:103
  121.8 1.5 %convolution_bitcast_fusion.2 = f32[1,4,128,128]{3,2,1,0:T(8,128)S(1)} fusion(f32[4,256,128]{2,1,0:T(8,128)S(1)} %copy-done.17, f32[4,256]{1,0:T(4,128)S(1)} %maximum_select_fusion.2, bf16[4,128,128]{2,1,0:T(8,128)(2,1)S(1)} %collective-permute-done.6, bf16[4,128,128]{2,1,0:T(8,128)(2,1)} %collective-permute-done.5, pred[]{:T(512)S(6)} %eq.4), kind=kOutput, calls=%fused_computation.58 | convolution fusion | flops 34996224 | bytes 1052673 | tf_op jit(solution)/shard_map/hqk,hqd->hkd/dot_general | solution.py:106
  124.6 2.3 %fusion.21 = f32[1,4,256,128]{3,2,1,0:T(8,128)} fusion(f32[4,256,256]{1,2,0:T(8,128)S(1)} %fusion.9, f32[4,256]{1,0:T(4,128)S(1)} %copy.237, bf16[3,4,256,1,128]{4,2,1,0,3:T(8,128)(2,1)S(1)} %fusion.5, bf16[3,4,256,128]{3,2,1,0:T(8,128)(2,1)} %collective-permute-done, bf16[4,256,128]{2,1,0:T(8,128)(2,1)} %collective-permute-done.10), kind=kOutput, calls=%fused_computation.42 | convolution fusion | flops 135135232 | bytes 2363392 | tf_op jit(solution)/shard_map/hqk,hqd->hkd/dot_general | solution.py:103
  127.4 1.4 fusion.6
  129.9 2.4 %copy.245 = f32[3,4,512,128]{2,3,1,0:T(8,128)} copy(f32[3,4,512,128]{3,2,1,0:T(8,128)S(1)} %bitcast.145) | data formatting | bytes 6291456 | tf_op jit(solution)/shard_map/mul | solution.py:230
  132.3 3.3 %fusion.3 = bf16[3,512,4,128]{1,3,2,0:T(8,128)(2,1)S(1)} fusion(f32[3,4,512,128]{2,3,1,0:T(8,128)} %copy.245, f32[1,4,512,128]{2,3,1,0:T(8,128)} %convolution_bitcast_fusion, f32[1,4,512,128]{2,3,1,0:T(8,128)} %fusion.12, f32[1,4,512,128]{2,3,1,0:T(8,128)} %fusion.11), kind=kLoop, calls=%fused_computation.12 | loop fusion | flops 3145728 | bytes 7864320 | tf_op jit(solution)/shard_map/transpose | solution.py:231
  (122 shorter events, 37.4 us)
Async XLA Ops:
  0.6 1.7 %copy-start.18 = (bf16[512,512]{1,0:T(8,128)(2,1)S(1)}, bf16[512,512]{1,0:T(8,128)(2,1)}, u32[]{:S(2)}) copy-start(bf16[512,512]{1,0:T(8,128)(2,1)} %param.5) | copy-start | bytes 1572868
  0.6 2.3 %copy-start.19 = (bf16[512,512]{1,0:T(8,128)(2,1)S(1)}, bf16[512,512]{1,0:T(8,128)(2,1)}, u32[]{:S(2)}) copy-start(bf16[512,512]{1,0:T(8,128)(2,1)} %param.4) | copy-start | bytes 1572868
  2.0 0.9 copy-start.8
  3.2 16.4 %copy-start.2 = (bf16[512,512]{0,1:T(8,128)(2,1)}, bf16[512,512]{0,1:T(8,128)(2,1)S(1)}, u32[]{:S(2)}) copy-start(bf16[512,512]{0,1:T(8,128)(2,1)S(1)} %copy.186) | copy-start | bytes 1572868
  5.6 16.7 %copy-start.14 = (bf16[3,4,128,1,128]{4,2,1,0,3:T(8,128)(2,1)}, bf16[3,4,128,1,128]{4,2,1,0,3:T(8,128)(2,1)S(1)}, u32[]{:S(2)}) copy-start(bf16[3,4,128,1,128]{4,2,1,0,3:T(8,128)(2,1)S(1)} %multiply_convert_fusion.2) | copy-start | bytes 1179652
  5.6 12.3 %collective-permute-start.1 = (bf16[3,4,128,128]{3,2,1,0:T(8,128)(2,1)S(1)}, bf16[3,4,128,128]{3,2,1,0:T(8,128)(2,1)}, u32[]{:S(2)}, u32[]{:S(2)}) collective-permute-start(bf16[3,4,128,128]{3,2,1,0:T(8,128)(2,1)S(1)} %bitcast.173), channel_id=1, source_target_pairs={{0,4},{2,6},{4,0},{6,2},{8,12},{10,14},{12,8},{14,10},{16,20},{18,... | collective-permute-start | bytes 1179656 | tf_op jit(solution)/shard_map/ppermute | solution.py:19
  9.7 32.9 %collective-permute-start = (bf16[3,4,256,128]{3,2,1,0:T(8,128)(2,1)}, bf16[3,4,256,128]{3,2,1,0:T(8,128)(2,1)}, u32[]{:S(2)}, u32[]{:S(2)}) collective-permute-start(bf16[3,4,256,128]{3,2,1,0:T(8,128)(2,1)} %fusion.99), channel_id=1, source_target_pairs={{0,2},{2,0},{4,6},{6,4},{8,10},{10,8},{12,14},{14,12},{16,18},{18,... | collective-permute-start | bytes 2359304 | tf_op jit(solution)/shard_map/ppermute | solution.py:19
  17.9 19.6 %collective-permute-start.2 = (bf16[3,4,128,128]{3,2,1,0:T(8,128)(2,1)}, bf16[3,4,128,128]{3,2,1,0:T(8,128)(2,1)}, u32[]{:S(2)}, u32[]{:S(2)}) collective-permute-start(bf16[3,4,128,128]{3,2,1,0:T(8,128)(2,1)} %collective-permute-done.1), channel_id=1, source_target_pairs={{0,2},{2,0},{4,6},{6,4},{8,10},{10,8},{12,14},{14,12},{16,18},{18,... | collective-permute-start | bytes 1179656 | tf_op jit(solution)/shard_map/ppermute | solution.py:19
  22.3 6.6 %copy-start.20 = (bf16[512,512]{1,0:T(8,128)(2,1)S(1)}, bf16[512,512]{1,0:T(8,128)(2,1)}, u32[]{:S(2)}) copy-start(bf16[512,512]{1,0:T(8,128)(2,1)} %param.7) | copy-start | bytes 1572868
  26.2 13.2 %copy-start.21 = (f32[4,512]{1,0:T(4,128)}, f32[4,512]{1,0:T(4,128)S(1)}, u32[]{:S(2)}) copy-start(f32[4,512]{1,0:T(4,128)S(1)} %fusion.1) | copy-start | bytes 24580
  26.2 12.9 %copy-start.15 = (bf16[3,4,128,1,128]{4,2,1,0,3:T(8,128)(2,1)S(1)}, bf16[3,4,128,1,128]{4,2,1,0,3:T(8,128)(2,1)}, u32[]{:S(2)}) copy-start(bf16[3,4,128,1,128]{4,2,1,0,3:T(8,128)(2,1)} %copy-done.14) | copy-start | bytes 1179652
  39.1 3.6 %copy-start.6 = (bf16[3,4,256,128]{3,2,1,0:T(8,128)(2,1)}, bf16[3,4,256,128]{3,2,1,0:T(8,128)(2,1)S(1)}, u32[]{:S(2)}) copy-start(bf16[3,4,256,128]{3,2,1,0:T(8,128)(2,1)S(1)} %maximum_select_fusion) | copy-start | bytes 2359300
  39.4 3.2 %copy-start.4 = (f32[4,128,256]{2,1,0:T(8,128)}, f32[4,128,256]{2,1,0:T(8,128)S(1)}, u32[]{:S(2)}) copy-start(f32[4,128,256]{2,1,0:T(8,128)S(1)} %get-tuple-element.47) | copy-start | bytes 1572868
  39.4 64.3 %collective-permute-start.3 = (f32[4,128]{1,0:T(4,128)S(1)}, f32[4,128]{1,0:T(4,128)}, u32[]{:S(2)}, u32[]{:S(2)}) collective-permute-start(f32[4,128]{1,0:T(4,128)S(1)} %get-tuple-element.46), channel_id=1, source_target_pairs={{0,4},{2,6},{4,0},{6,2},{8,12},{10,14},{12,8},{14,10},{16,20},{18,... | collective-permute-start | bytes 6152 | tf_op jit(solution)/shard_map/ppermute | solution.py:19
  44.1 71.5 %collective-permute-start.9 = (f32[4,256]{1,0:T(4,128)S(1)}, f32[4,256]{1,0:T(4,128)}, u32[]{:S(2)}, u32[]{:S(2)}) collective-permute-start(f32[4,256]{1,0:T(4,128)S(1)} %get-tuple-element.48), channel_id=1, source_target_pairs={{0,2},{2,0},{4,6},{6,4},{8,10},{10,8},{12,14},{14,12},{16,18},{18,... | collective-permute-start | bytes 12296 | tf_op jit(solution)/shard_map/ppermute | solution.py:19
  60.2 4.3 %copy-start = (f32[4,512,512]{1,2,0:T(8,128)S(1)}, f32[4,512,512]{1,2,0:T(8,128)}, u32[]{:S(2)}) copy-start(f32[4,512,512]{1,2,0:T(8,128)} %get-tuple-element.51) | copy-start | bytes 12582916
  60.3 4.3 %copy-start.9 = (bf16[512,512]{0,1:T(8,128)(2,1)S(1)}, bf16[512,512]{0,1:T(8,128)(2,1)}, u32[]{:S(2)}) copy-start(bf16[512,512]{0,1:T(8,128)(2,1)} %copy-done.8) | copy-start | bytes 1572868
  67.9 7.6 %copy-start.22 = (f32[4,256]{1,0:T(4,128)S(1)}, f32[4,256]{1,0:T(4,128)}, u32[]{:S(2)}) copy-start(f32[4,256]{1,0:T(4,128)} %fusion.40) | copy-start | bytes 12292
  76.9 4.8 %copy-start.1 = (f32[4,512,512]{1,2,0:T(8,128)S(1)}, f32[4,512,512]{1,2,0:T(8,128)}, u32[]{:S(2)}) copy-start(f32[4,512,512]{1,2,0:T(8,128)} %get-tuple-element.51) | copy-start | bytes 12582916
  76.9 4.8 %copy-start.7 = (bf16[4,512,128]{2,1,0:T(8,128)(2,1)S(1)}, bf16[4,512,128]{2,1,0:T(8,128)(2,1)}, u32[]{:S(2)}) copy-start(bf16[4,512,128]{2,1,0:T(8,128)(2,1)} %get-tuple-element.52) | copy-start | bytes 1572868
  76.9 4.8 %copy-start.10 = (bf16[512,512]{0,1:T(8,128)(2,1)S(1)}, bf16[512,512]{0,1:T(8,128)(2,1)}, u32[]{:S(2)}) copy-start(bf16[512,512]{0,1:T(8,128)(2,1)} %copy-done.8) | copy-start | bytes 1572868
  81.7 1.9 %copy-start.3 = (bf16[512,512]{0,1:T(8,128)(2,1)S(1)}, bf16[512,512]{0,1:T(8,128)(2,1)}, u32[]{:S(2)}) copy-start(bf16[512,512]{0,1:T(8,128)(2,1)} %copy-done.2) | copy-start | bytes 1572868
  85.4 6.1 %copy-start.11 = (f32[4,256,2]{0,2,1:T(2,128)S(1)}, f32[4,256,2]{0,2,1:T(2,128)}, u32[]{:S(2)}) copy-start(f32[4,256,2]{0,2,1:T(2,128)} %broadcast_in_dim.53) | copy-start | bytes 24580
  85.4 6.2 %copy-start.12 = (f32[4,256,2]{0,2,1:T(2,128)S(1)}, f32[4,256,2]{0,2,1:T(2,128)}, u32[]{:S(2)}) copy-start(f32[4,256,2]{0,2,1:T(2,128)} %broadcast_in_dim.24.clone) | copy-start | bytes 24580
  85.4 7.7 %copy-start.23 = (f32[4,128,4]{1,2,0:T(4,128)S(1)}, f32[4,128,4]{1,2,0:T(4,128)}, u32[]{:S(2)}) copy-start(f32[4,128,4]{1,2,0:T(4,128)} %copy.215) | copy-start | bytes 24580
  86.9 11.1 %copy-start.16 = (f32[4,512]{0,1:T(8,128)S(1)}, f32[4,512]{0,1:T(8,128)}, u32[]{:S(2)}) copy-start(f32[4,512]{0,1:T(8,128)} %copy.230) | copy-start | bytes 24580
  86.9 18.6 %copy-start.5 = (f32[4,128,256]{2,1,0:T(8,128)S(1)}, f32[4,128,256]{2,1,0:T(8,128)}, u32[]{:S(2)}) copy-start(f32[4,128,256]{2,1,0:T(8,128)} %copy-done.4) | copy-start | bytes 1572868
  88.8 26.1 %collective-permute-start.5 = (bf16[4,128,128]{2,1,0:T(8,128)(2,1)S(1)}, bf16[4,128,128]{2,1,0:T(8,128)(2,1)}, u32[]{:S(2)}, u32[]{:S(2)}) collective-permute-start(bf16[4,128,128]{2,1,0:T(8,128)(2,1)S(1)} %reduce_sum.107), channel_id=1, source_target_pairs={{0,4},{2,6},{4,0},{6,2},{8,12},{10,14},{12,8},{14,10},{16,20},{18,... | collective-permute-start | bytes 393224 | tf_op jit(solution)/shard_map/ppermute | solution.py:19
  93.1 14.6 %copy-start.13 = (bf16[512,4,128]{2,0,1:T(8,128)(2,1)S(1)}, bf16[512,4,128]{2,0,1:T(8,128)(2,1)}, u32[]{:S(2)}) copy-start(bf16[512,4,128]{2,0,1:T(8,128)(2,1)} %get-tuple-element.43) | copy-start | bytes 1572868
  94.5 14.4 %collective-permute-start.7 = (f32[4,128]{1,0:T(4,128)}, f32[4,128]{1,0:T(4,128)}, u32[]{:S(2)}, u32[]{:S(2)}) collective-permute-start(f32[4,128]{1,0:T(4,128)} %multiply_reduce_fusion.2), channel_id=1, source_target_pairs={{0,4},{2,6},{4,0},{6,2},{8,12},{10,14},{12,8},{14,10},{16,20},{18,... | collective-permute-start | bytes 6152 | tf_op jit(solution)/shard_map/ppermute | solution.py:19
  97.5 25.8 %collective-permute-start.10 = (bf16[4,256,128]{2,1,0:T(8,128)(2,1)S(1)}, bf16[4,256,128]{2,1,0:T(8,128)(2,1)}, u32[]{:S(2)}, u32[]{:S(2)}) collective-permute-start(bf16[4,256,128]{2,1,0:T(8,128)(2,1)S(1)} %reduce_sum.111), channel_id=1, source_target_pairs={{0,2},{2,0},{4,6},{6,4},{8,10},{10,8},{12,14},{14,12},{16,18},{18,... | collective-permute-start | bytes 786440 | tf_op jit(solution)/shard_map/ppermute | solution.py:19
  103.7 5.5 %collective-permute-start.4 = (f32[4,128]{1,0:T(4,128)}, f32[4,128]{1,0:T(4,128)S(1)}, u32[]{:S(2)}, u32[]{:S(2)}) collective-permute-start(f32[4,128]{1,0:T(4,128)} %collective-permute-done.3), channel_id=1, source_target_pairs={{0,2},{2,0},{4,6},{6,4},{8,10},{10,8},{12,14},{14,12},{16,18},{18,... | collective-permute-start | bytes 6152 | tf_op jit(solution)/shard_map/ppermute | solution.py:19
  106.9 13.2 %copy-start.17 = (f32[4,256,128]{2,1,0:T(8,128)S(1)}, f32[4,256,128]{2,1,0:T(8,128)}, u32[]{:S(2)}) copy-start(f32[4,256,128]{2,1,0:T(8,128)} %convolution_multiply_fusion.5) | copy-start | bytes 1572868
  108.9 7.9 %collective-permute-start.11 = (f32[4,256]{0,1:T(8,128)}, f32[4,256]{0,1:T(8,128)S(1)}, u32[]{:S(2)}, u32[]{:S(2)}) collective-permute-start(f32[4,256]{0,1:T(8,128)} %copy.267), channel_id=1, source_target_pairs={{0,2},{2,0},{4,6},{6,4},{8,10},{10,8},{12,14},{14,12},{16,18},{18,... | collective-permute-start | bytes 12296 | tf_op jit(solution)/shard_map/ppermute | solution.py:19
  109.2 4.9 %collective-permute-start.8 = (f32[4,128]{1,0:T(4,128)}, f32[4,128]{1,0:T(4,128)S(1)}, u32[]{:S(2)}, u32[]{:S(2)}) collective-permute-start(f32[4,128]{1,0:T(4,128)} %collective-permute-done.7), channel_id=1, source_target_pairs={{0,2},{2,0},{4,6},{6,4},{8,10},{10,8},{12,14},{14,12},{16,18},{18,... | collective-permute-start | bytes 6152 | tf_op jit(solution)/shard_map/ppermute | solution.py:19
  114.9 5.2 %collective-permute-start.6 = (bf16[4,128,128]{2,1,0:T(8,128)(2,1)}, bf16[4,128,128]{2,1,0:T(8,128)(2,1)S(1)}, u32[]{:S(2)}, u32[]{:S(2)}) collective-permute-start(bf16[4,128,128]{2,1,0:T(8,128)(2,1)} %collective-permute-done.5), channel_id=1, source_target_pairs={{0,2},{2,0},{4,6},{6,4},{8,10},{10,8},{12,14},{14,12},{16,18},{18,... | collective-permute-start | bytes 393224 | tf_op jit(solution)/shard_map/ppermute | solution.py:19
where the time goes:
time: 140 us; the launch traced here: 139 us
  local copies, waits for them, and re-layouts  46.4 us (33%)
  matrix products  33.2 us (24%)
  other arithmetic  26.5 us (19%)
  starting transfers between devices  15.2 us (11%)
  waiting for transfers between devices  13.8 us (10%)
  blocking collectives  2.62 us (2%)
    ppermute x12, starting transfers between devices, from_partner(): return lax.ppermute(value, axis, pairs)  15.2 us
    ppermute x12, waiting for transfers between devices, from_partner(): return lax.ppermute(value, axis, pairs)  13.8 us
    unnamed x58, local copies, waits for them, and re-layouts  7.04 us
    dot_general x3, matrix products, attend(): jnp.einsum('hgqk,hgkd->hgqd', rounded, value_blocks, preferred_element_ty...  6.14 us
    dot_general x1, matrix products, attend_back(): jnp.einsum('hgqk,hgqd->hgkd', rounded, grad_blocks, preferred_element_typ...  4.8 us
    reduce_sum x3, other arithmetic, shards(): exp_scores.sum(-1).reshape(head_count, level_rows)  4.46 us
    reduce_sum x2, other arithmetic, shards(): gathered_grad = (share_of[..., None] * grad_attended).reshape(head_count,...  4.43 us
    dot_general x3, matrix products, attend(): jnp.einsum('hgqd,hgkd->hgqk', query_blocks, key_blocks, preferred_element...  4.31 us
  transfers between devices with their start and end apart: 12, of which 4 were waited for; matrix products, arithmetic and copies ran while one was open for 62% of the time, Pallas kernels for 0%

commit v1 on v0

v1 whole, which is shorter than its diff:
```python
import functools

import jax
import jax.numpy as jnp
from jax import lax
from jax.experimental import pallas as pl
from jax.experimental.pallas import tpu as pltpu
from jax.sharding import PartitionSpec as P

DH = 128
LEAF = 256
EPSILON = 1e-06
SCALE = DH ** (-0.5)
LOG2 = SCALE * 1.4426950408889634
MESH = pl.DeviceIdType.MESH
F32 = jnp.float32
BF16 = jnp.bfloat16
PACK = DH + 16


def nn(a, b):
    return lax.dot_general(a, b, (((1,), (0,)), ((), ())), preferred_element_type=F32)


def nt(a, b):
    return lax.dot_general(a, b, (((1,), (1,)), ((), ())), preferred_element_type=F32)


def wide(x):
    return x.astype(F32)


def flip(x):
    return wide(x).T.astype(BF16)


def halve(x):
    half = x.shape[0] // 2
    return ((wide(x[:half]) + wide(x[half:])) * 0.5).astype(BF16)


def twice(x, axis):
    return jnp.concatenate([x, x], axis)


def fold(x):
    half = x.shape[1] // 2
    return x[:, :half] + x[:, half:]


def packed_rows(first, second, third):
    row = lax.broadcasted_iota(jnp.int32, (16, first.shape[1]), 0)
    return jnp.where(row == 0, first, jnp.where(row == 1, second, jnp.where(row == 2, third, 0.0))).astype(BF16)


def kernel(
    q_ref, k_ref, v_ref, g_ref,
    no_ref, gq_ref, gk_ref, gv_ref,
    perm, back, qs, ks, vs, kts, vts, dos, p0, p1, p2, a0, a1, rows, att,
    q1, kv1, kv1p, k2c, v2c, q2, q2v, a2o, a2i, xo, xi,
    g0, g1, g2o, g2i, dq1, dq2o, dq2i, dkvo, dkvi, dkv0, dkv2,
    send, recv,
):
    tokens, width = q_ref.shape
    heads = width // DH
    half, quarter = tokens // 2, tokens // 4
    full_width = width * 2
    seq, core = lax.axis_index("seq"), lax.axis_index("head")
    at_x = (seq + 1 - 2 * (seq % 2), core)
    at_y = (seq + 2 - 4 * ((seq // 2) % 2), core)
    at_core = (seq, 1 - core)

    def copy(kind, h, source, target, where):
        return pltpu.make_async_remote_copy(
            src_ref=source, dst_ref=target, send_sem=send.at[kind, h], recv_sem=recv.at[kind, h],
            device_id=where, device_id_type=MESH,
        )

    def kv_copy(h):
        return copy(0, h, kv1.at[h], kv1p.at[h], at_x)

    def q2_copy(h):
        return copy(1, h, q2.at[h], q2v.at[h], at_y)

    def a2_copy(h):
        return copy(2, h, a2o.at[h], a2i.at[h], at_y)

    def g2_copy(h):
        return copy(3, h, g2o.at[h], g2i.at[h], at_y)

    def dkv_copy(h):
        return copy(4, h, dkvo.at[h], dkvi.at[h], at_x)

    def dq2_copy(h):
        return copy(5, h, dq2o.at[h], dq2i.at[h], at_y)

    def x_copy():
        return copy(6, 0, xo, xi, at_core)

    def cols(h):
        return pl.ds(pl.multiple_of(h * DH, DH), DH)

    def each_head(body):
        @pl.loop(0, heads)
        def _(h):
            body(h)

    barrier = pltpu.get_barrier_semaphore()
    for where in (at_x, at_y, at_core):
        pl.semaphore_signal(barrier, inc=1, device_id=where, device_id_type=MESH)

    def order(p):
        slab = p // quarter
        return 4 * (p % quarter) + slab // 2 + 2 * (slab % 2)

    shape = (tokens, tokens)
    major = lax.broadcasted_iota(jnp.int32, shape, 0)
    minor = lax.broadcasted_iota(jnp.int32, shape, 1)
    perm[...] = jnp.where(order(major) == minor, 1.0, 0.0).astype(BF16)
    pl.semaphore_wait(barrier, 3)

    def load_kv(h):
        for n, (ref, kept) in enumerate(((k_ref, ks), (v_ref, vs))):
            moved = nn(perm[...], ref[:, cols(h)])
            kept[h] = moved.astype(BF16)
            kv1[h, n] = halve(moved)
        kv_copy(h).start()

    each_head(load_kv)

    def load_q(h):
        moved = nn(perm[...], q_ref[:, cols(h)])
        qs[h] = moved.astype(BF16)
        first = halve(moved)
        q1[h] = first
        q2[h] = halve(first)
        q2_copy(h).start()

    each_head(load_q)

    def softmax(scores):
        top = jnp.max(scores, axis=0, keepdims=True)
        e = jnp.exp2((scores - top) * LOG2)
        return top * LOG2, jnp.sum(e, axis=0, keepdims=True), e.astype(BF16)

    def level0(h):
        kts[h] = flip(ks[h])
        vt = flip(vs[h])
        m, s, p = softmax(nt(ks[h], qs[h]))
        p0[h] = p
        a0[h] = nn(vt, p)
        rows[h, 0:1, :] = m
        rows[h, 1:2, :] = s
        dos[h] = nn(perm[...], g_ref[:, cols(h)]).T.astype(BF16)

    each_head(level0)
    back[...] = jnp.where(order(minor) == major, 1.0, 0.0).astype(BF16)

    def coarse(h):
        kv_copy(h).wait_recv()
        q2_copy(h).wait_recv()
        k1p, v1p = kv1p[h, 0], kv1p[h, 1]
        k2 = jnp.concatenate([halve(kv1[h, 0]), halve(k1p)], 0)
        v2 = jnp.concatenate([halve(kv1[h, 1]), halve(v1p)], 0)
        k2c[h] = k2
        v2c[h] = v2
        scores = nt(k2, q2v[h]) * LOG2
        m = wide(jnp.max(scores, axis=0, keepdims=True).astype(BF16))
        e = jnp.exp2(scores - m)
        s = jnp.sum(e, axis=0, keepdims=True)
        p = e.astype(BF16)
        p2[h] = p
        a2o[h, 0:DH] = nn(flip(v2), p).astype(BF16)
        high = wide(s.astype(BF16))
        a2o[h, DH:PACK] = packed_rows(m, high, s - high)
        a2_copy(h).start()
        m, s, p = softmax(nt(k1p, q1[h]))
        p1[h] = p
        a1[h] = nn(flip(v1p), p)
        rows[h, 2:3, :] = twice(m, 1)
        rows[h, 3:4, :] = twice(s, 1)

    def combine(h):
        a2_copy(h).wait_recv()
        m0, s0 = rows[h, 0:1, :], rows[h, 1:2, :]
        m1, s1 = rows[h, 2:3, :], rows[h, 3:4, :]
        figures = wide(a2i[h, DH:PACK])
        m2 = twice(twice(figures[0:1], 1), 1)
        s2 = twice(twice(figures[1:2] + figures[2:3], 1), 1)
        top = jnp.maximum(jnp.maximum(m0, m1), m2)
        f0 = jnp.exp2(m0 - top)
        f1 = 2.0 * jnp.exp2(m1 - top)
        f2 = 4.0 * jnp.exp2(m2 - top)
        den = 1.0 / (f0 * s0 + f1 * s1 + f2 * s2)
        w0, w1, w2 = f0 * den, f1 * den, f2 * den
        a2 = wide(a2i[h, 0:DH])
        attended = w0 * a0[h] + w1 * twice(a1[h], 1) + w2 * twice(twice(a2, 1), 1)
        rounded = attended.astype(BF16)
        att[h] = rounded
        attended = wide(rounded)
        rows[h, 0:1, :] = w0
        rows[h, 1:2, :] = w1
        rows[h, 2:3, :] = w2
        squares = jnp.sum(attended * attended, axis=0, keepdims=True)
        dots = jnp.sum(attended * wide(dos[h]), axis=0, keepdims=True)
        rows[h, 3:4, :] = squares
        rows[h, 4:5, :] = dots
        xo[0:1, :] += squares
        xo[1:2, :] += dots

    xo[...] = jnp.zeros_like(xo)
    coarse(0)

    @pl.loop(1, heads)
    def _(h):
        coarse(h)
        combine(h - 1)

    combine(heads - 1)
    x_copy().start()
    x_copy().wait_recv()
    inverse = lax.rsqrt((xo[0:1, :] + xi[0:1, :]) / full_width + EPSILON)
    pull = inverse * inverse * inverse * (xo[1:2, :] + xi[1:2, :]) / full_width

    def cotangents(h):
        w0, w1, w2 = rows[h, 0:1, :], rows[h, 1:2, :], rows[h, 2:3, :]
        grad = inverse * wide(dos[h]) - pull * wide(att[h])
        along = inverse * rows[h, 4:5, :] - pull * rows[h, 3:4, :]
        g2o[h, 0:DH] = fold(fold(w2 * grad)).astype(BF16)
        delta = fold(fold(w2 * along))
        high = wide(delta.astype(BF16))
        g2o[h, DH:PACK] = packed_rows(high, delta - high, delta * 0.0)
        g2_copy(h).start()
        g0[h] = (w0 * grad).astype(BF16)
        g1[h] = fold(w1 * grad).astype(BF16)
        rows[h, 5:6, :] = w0 * along
        rows[h, 6:7, :] = twice(fold(w1 * along), 1)

    each_head(cotangents)

    def score_grads(p, values, grads, delta):
        return (wide(p) * (nn(values, grads) - delta)).astype(BF16)

    def coarse_back(h):
        k1p, v1p = kv1p[h, 0], kv1p[h, 1]
        ds = score_grads(p1[h], v1p, g1[h], rows[h, 6:7, 0:half])
        dk = nn(ds, q1[h])
        dv = nt(p1[h], g1[h])
        dq1[h] = nn(flip(k1p), ds)
        g2_copy(h).wait_recv()
        figures = wide(g2i[h, DH:PACK])
        grads = g2i[h, 0:DH]
        ds = score_grads(p2[h], v2c[h], grads, figures[0:1] + figures[1:2])
        dk2 = nn(ds, q2v[h])
        dv2 = nt(p2[h], grads)
        dq2o[h] = nn(flip(k2c[h]), ds).astype(BF16)
        dq2_copy(h).start()
        dkvo[h, 0] = ((dk + 0.5 * twice(dk2[quarter:], 0)) * SCALE).astype(BF16)
        dkvo[h, 1] = (dv + 0.5 * twice(dv2[quarter:], 0)).astype(BF16)
        dkv_copy(h).start()
        dkv2[h, 0] = dk2[:quarter] * SCALE
        dkv2[h, 1] = dv2[:quarter]

    each_head(coarse_back)

    def level0_back(h):
        no_ref[:, cols(h)] = nt(back[...], (wide(att[h]) * inverse).astype(BF16)).astype(BF16)
        ds = score_grads(p0[h], vs[h], g0[h], rows[h, 5:6, :])
        dkv0[h, 0] = nn(ds, qs[h]) * SCALE
        dkv0[h, 1] = nt(p0[h], g0[h])
        dq = nn(kts[h], ds) + 0.5 * twice(dq1[h], 1)
        dq2_copy(h).wait_recv()
        dq = (dq + 0.25 * twice(twice(wide(dq2i[h]), 1), 1)) * SCALE
        gq_ref[:, cols(h)] = nt(back[...], dq.astype(BF16)).astype(BF16)

    each_head(level0_back)

    def finish(h):
        dkv_copy(h).wait_recv()
        for n, out in enumerate((gk_ref, gv_ref)):
            total = (
                dkv0[h, n] + 0.5 * twice(wide(dkvi[h, n]), 0) + 0.25 * twice(twice(dkv2[h, n], 0), 0)
            )
            out[:, cols(h)] = nn(back[...], total.astype(BF16)).astype(BF16)

    each_head(finish)

    def drain(h):
        for make in (kv_copy, q2_copy, a2_copy, g2_copy, dkv_copy, dq2_copy):
            make(h).wait_send()

    each_head(drain)
    x_copy().wait_send()


def shards(queries, key_states, value_states, out_grad):
    tokens, width = queries.shape
    heads = width // DH
    half, quarter = tokens // 2, tokens // 4

    def vmem(*shape, dtype=BF16):
        return pltpu.VMEM(shape, dtype)

    scratch = [
        vmem(tokens, tokens), vmem(tokens, tokens),
        vmem(heads, tokens, DH), vmem(heads, tokens, DH), vmem(heads, tokens, DH),
        vmem(heads, DH, tokens), vmem(heads, DH, tokens), vmem(heads, DH, tokens),
        vmem(heads, tokens, tokens), vmem(heads, half, half), vmem(heads, half, quarter),
        vmem(heads, DH, tokens, dtype=F32), vmem(heads, DH, half, dtype=F32),
        vmem(heads, 8, tokens, dtype=F32), vmem(heads, DH, tokens),
        vmem(heads, half, DH), vmem(heads, 2, half, DH), vmem(heads, 2, half, DH),
        vmem(heads, half, DH), vmem(heads, half, DH),
        vmem(heads, quarter, DH), vmem(heads, quarter, DH),
        vmem(heads, PACK, quarter), vmem(heads, PACK, quarter),
        vmem(8, tokens, dtype=F32), vmem(8, tokens, dtype=F32),
        vmem(heads, DH, tokens), vmem(heads, DH, half),
        vmem(heads, PACK, quarter), vmem(heads, PACK, quarter),
        vmem(heads, DH, half, dtype=F32),
        vmem(heads, DH, quarter), vmem(heads, DH, quarter),
        vmem(heads, 2, half, DH), vmem(heads, 2, half, DH),
        vmem(heads, 2, tokens, DH, dtype=F32), vmem(heads, 2, quarter, DH, dtype=F32),
        pltpu.SemaphoreType.DMA((7, heads)),
        pltpu.SemaphoreType.DMA((7, heads)),
    ]
    flops = 2 * heads * DH * tokens * tokens * 12
    return pl.pallas_call(
        kernel,
        out_shape=[jax.ShapeDtypeStruct((tokens, width), BF16)] * 4,
        in_specs=[pl.BlockSpec(memory_space=pltpu.VMEM)] * 4,
        out_specs=[pl.BlockSpec(memory_space=pltpu.VMEM)] * 4,
        scratch_shapes=scratch,
        compiler_params=pltpu.CompilerParams(
            collective_id=0, has_side_effects=True, vmem_limit_bytes=48 * 1024 * 1024
        ),
        cost_estimate=pl.CostEstimate(
            flops=flops, bytes_accessed=16 * tokens * width, transcendentals=heads * tokens * tokens
        ),
        name="hierarchical_attention",
    )(queries, key_states, value_states, out_grad)


def solution(mesh):
    return jax.shard_map(
        shards,
        mesh=mesh,
        in_specs=(P("seq", "head"),) * 4,
        out_specs=(P("seq", "head"),) * 4,
        check_vma=False,
    )
```

time: 140 us -> 45.8 us (0.33)
  local copies, waits for them, and re-layouts: 46.4 us -> 7.33 us
  Pallas kernels: 0 us -> 37.5 us
  matrix products: 33.2 us -> 0 us
  other arithmetic: 26.5 us -> 0 us
  starting transfers between devices: 15.2 us -> 0 us
  waiting for transfers between devices: 13.8 us -> 0 us
  blocking collectives: 2.62 us -> 0 us
    pallas_call x0 -> x1, Pallas kernels: none -> 37.5 us  [shards(): pl.pallas_call(kernel, out_shape=[jax.ShapeDtypeStruct((tokens, width), B...]
    dot_general x18 -> x0, matrix products: 33.2 us -> none  [the longest x3 6.14 us: attend(): jnp.einsum('hgqk,hgkd->hgqd', rounded, value_blocks, preferred_element_ty...]
    ppermute x12 -> x0, starting transfers between devices: 15.2 us -> none  [from_partner(): return lax.ppermute(value, axis, pairs)]
    ppermute x12 -> x0, waiting for transfers between devices: 13.8 us -> none  [from_partner(): return lax.ppermute(value, axis, pairs)]
    reduce_sum x7 -> x0, other arithmetic: 11.1 us -> none  [the longest x3 4.46 us: shards(): exp_scores.sum(-1).reshape(head_count, level_rows)]
    broadcast_in_dim x11 -> x0, local copies, waits for them, and re-layouts: 9.81 us -> none  [the longest x3 4.1 us: shards(): jnp.repeat(exp_scores.sum(-1).reshape(head_count, level_rows), stretch, a...]
    another operation x9 -> x0, local copies, waits for them, and re-layouts: 8.79 us -> none  [the longest x3 4.29 us: shards(): maxima_up.append(jnp.repeat(row_maxima, stretch, axis=1))]
    mul x6 -> x0, other arithmetic: 6.47 us -> none  [the longest x1 3.19 us: shards(): share_of[..., None] * grad_attended]
  transfers between devices with their start and end apart: 12 -> 0, of which waited for: 4 -> 0; matrix products, arithmetic and copies ran while one was open for 62% -> 0% of each run, Pallas kernels for 0% -> 0%
where the time goes in v1:
time: 45.8 us; the launch traced here: 45.5 us
  Pallas kernels  37.5 us (82%)
  local copies, waits for them, and re-layouts  7.33 us (16%)
  between operations  0.65 us (1%)
    pallas_call x1, Pallas kernels, shards(): pl.pallas_call(kernel, out_shape=[jax.ShapeDtypeStruct((tokens, width), B...  37.5 us
    unnamed x12, local copies, waits for them, and re-layouts  7.33 us

profile of v1, /device:TPU:0, one launch (start us, length us, event | category | flops | bytes accessed | tf_op | source)
XLA Modules:
  0.0 45.5 jit_solution(9893854891273667555)
XLA Ops:
  0.6 0.0 copy-start
  0.6 1.0 %copy-done = bf16[512,512]{1,0:T(8,128)(2,1)S(1)} copy-done((bf16[512,512]{1,0:T(8,128)(2,1)S(1)}, bf16[512,512]{1,0:T(8,128)(2,1)}, u32[]{:S(2)}) %copy-start) | copy-done | bytes 524312
  1.7 0.0 copy-start.1
  1.7 1.0 %copy-done.1 = bf16[512,512]{1,0:T(8,128)(2,1)S(1)} copy-done((bf16[512,512]{1,0:T(8,128)(2,1)S(1)}, bf16[512,512]{1,0:T(8,128)(2,1)}, u32[]{:S(2)}) %copy-start.1) | copy-done | bytes 524312
  2.7 0.0 copy-start.2
  2.7 1.0 %copy-done.2 = bf16[512,512]{1,0:T(8,128)(2,1)S(1)} copy-done((bf16[512,512]{1,0:T(8,128)(2,1)S(1)}, bf16[512,512]{1,0:T(8,128)(2,1)}, u32[]{:S(2)}) %copy-start.2) | copy-done | bytes 524312
  3.8 0.0 copy-start.3
  3.8 1.0 %copy-done.3 = bf16[512,512]{1,0:T(8,128)(2,1)S(1)} copy-done((bf16[512,512]{1,0:T(8,128)(2,1)S(1)}, bf16[512,512]{1,0:T(8,128)(2,1)}, u32[]{:S(2)}) %copy-start.3) | copy-done | bytes 524312
  4.8 37.5 %hierarchical_attention.1 = (bf16[512,512]{1,0:T(8,128)(2,1)S(1)}, bf16[512,512]{1,0:T(8,128)(2,1)S(1)}, bf16[512,512]{1,0:T(8,128)(2,1)S(1)}, bf16[512,512]{1,0:T(8,128)(2,1)S(1)}) custom-call(bf16[512,512]{1,0:T(8,128)(2,1)S(1)} %copy-done, bf16[512,512]{1,0:T(8,128)(2,1)S(1)} %copy-done.1, bf16[512,512]{1,0:T(8,128)(2,1)S(1)} %copy-done.2, ...), custom_call_target="tpu_custom_call" | custom-call | flops 3221225472 | bytes 4194304 | tf_op jit(solution)/shard_map/hierarchical_attention/pallas_call | solution.py:326
  42.3 0.8 %copy.12 = bf16[512,512]{1,0:T(8,128)(2,1)} copy(bf16[512,512]{1,0:T(8,128)(2,1)S(1)} %get-tuple-element.8) | data formatting | bytes 1048576
  43.1 0.8 %copy.13 = bf16[512,512]{1,0:T(8,128)(2,1)} copy(bf16[512,512]{1,0:T(8,128)(2,1)S(1)} %get-tuple-element.9) | data formatting | bytes 1048576
  43.9 0.8 %copy.14 = bf16[512,512]{1,0:T(8,128)(2,1)} copy(bf16[512,512]{1,0:T(8,128)(2,1)S(1)} %get-tuple-element.10) | data formatting | bytes 1048576
  44.7 0.8 %copy.15 = bf16[512,512]{1,0:T(8,128)(2,1)} copy(bf16[512,512]{1,0:T(8,128)(2,1)S(1)} %get-tuple-element.11) | data formatting | bytes 1048576
Async XLA Ops:
  0.6 1.0 %copy-start = (bf16[512,512]{1,0:T(8,128)(2,1)S(1)}, bf16[512,512]{1,0:T(8,128)(2,1)}, u32[]{:S(2)}) copy-start(bf16[512,512]{1,0:T(8,128)(2,1)} %q_ref.1) | copy-start | bytes 1572868
  1.7 1.0 %copy-start.1 = (bf16[512,512]{1,0:T(8,128)(2,1)S(1)}, bf16[512,512]{1,0:T(8,128)(2,1)}, u32[]{:S(2)}) copy-start(bf16[512,512]{1,0:T(8,128)(2,1)} %k_ref.1) | copy-start | bytes 1572868
  2.7 1.0 %copy-start.2 = (bf16[512,512]{1,0:T(8,128)(2,1)S(1)}, bf16[512,512]{1,0:T(8,128)(2,1)}, u32[]{:S(2)}) copy-start(bf16[512,512]{1,0:T(8,128)(2,1)} %v_ref.1) | copy-start | bytes 1572868
  3.8 1.0 %copy-start.3 = (bf16[512,512]{1,0:T(8,128)(2,1)S(1)}, bf16[512,512]{1,0:T(8,128)(2,1)}, u32[]{:S(2)}) copy-start(bf16[512,512]{1,0:T(8,128)(2,1)} %g_ref.1) | copy-start | bytes 1572868

commit v2 on v1

--- a/solution.py
+++ b/solution.py
@@ -15,6 +15,8 @@
 MESH = pl.DeviceIdType.MESH
 F32 = jnp.float32
 BF16 = jnp.bfloat16
+PIECES = 4
+VMEM = 60 * 1024 * 1024
 PACK = DH + 16
 
 
@@ -56,10 +58,11 @@
 def kernel(
     q_ref, k_ref, v_ref, g_ref,
     no_ref, gq_ref, gk_ref, gv_ref,
-    perm, back, qs, ks, vs, kts, vts, dos, p0, p1, p2, a0, a1, rows, att,
+    outs,
+    inq, ink, inv, ing, perm, back, qs, ks, vs, kts, vts, dos, p0, p1, p2, a0, a1, rows, att,
     q1, kv1, kv1p, k2c, v2c, q2, q2v, a2o, a2i, xo, xi,
     g0, g1, g2o, g2i, dq1, dq2o, dq2i, dkvo, dkvi, dkv0, dkv2,
-    send, recv,
+    send, recv, arrived, written,
 ):
     tokens, width = q_ref.shape
     heads = width // DH
@@ -105,9 +108,22 @@
         def _(h):
             body(h)
 
+    def fetch(n, h):
+        source, target = ((k_ref, ink), (v_ref, inv), (q_ref, inq), (g_ref, ing))[n]
+        return pltpu.make_async_copy(source.at[:, cols(h)], target.at[h], arrived.at[n, h])
+
+    def put(n, h):
+        target = (no_ref, gq_ref, gk_ref, gv_ref)[n]
+        return pltpu.make_async_copy(outs.at[n, h], target.at[:, cols(h)], written.at[n, h])
+
     barrier = pltpu.get_barrier_semaphore()
     for where in (at_x, at_y, at_core):
         pl.semaphore_signal(barrier, inc=1, device_id=where, device_id_type=MESH)
+
+    for group in ((0, 1), (2, 3)):
+        for h in range(heads):
+            for n in group:
+                fetch(n, h).start()
 
     def order(p):
         slab = p // quarter
@@ -120,8 +136,9 @@
     pl.semaphore_wait(barrier, 3)
 
     def load_kv(h):
-        for n, (ref, kept) in enumerate(((k_ref, ks), (v_ref, vs))):
-            moved = nn(perm[...], ref[:, cols(h)])
+        for n, (ref, kept) in enumerate(((ink, ks), (inv, vs))):
+            fetch(n, h).wait()
+            moved = nn(perm[...], ref[h])
             kept[h] = moved.astype(BF16)
             kv1[h, n] = halve(moved)
         kv_copy(h).start()
@@ -129,7 +146,8 @@
     each_head(load_kv)
 
     def load_q(h):
-        moved = nn(perm[...], q_ref[:, cols(h)])
+        fetch(2, h).wait()
+        moved = nn(perm[...], inq[h])
         qs[h] = moved.astype(BF16)
         first = halve(moved)
         q1[h] = first
@@ -151,7 +169,8 @@
         a0[h] = nn(vt, p)
         rows[h, 0:1, :] = m
         rows[h, 1:2, :] = s
-        dos[h] = nn(perm[...], g_ref[:, cols(h)]).T.astype(BF16)
+        fetch(3, h).wait()
+        dos[h] = nn(perm[...], ing[h]).T.astype(BF16)
 
     each_head(level0)
     back[...] = jnp.where(order(minor) == major, 1.0, 0.0).astype(BF16)
@@ -264,33 +283,54 @@
     each_head(coarse_back)
 
     def level0_back(h):
-        no_ref[:, cols(h)] = nt(back[...], (wide(att[h]) * inverse).astype(BF16)).astype(BF16)
+        outs[0, h] = nt(back[...], (wide(att[h]) * inverse).astype(BF16)).astype(BF16)
+        put(0, h).start()
         ds = score_grads(p0[h], vs[h], g0[h], rows[h, 5:6, :])
         dkv0[h, 0] = nn(ds, qs[h]) * SCALE
         dkv0[h, 1] = nt(p0[h], g0[h])
         dq = nn(kts[h], ds) + 0.5 * twice(dq1[h], 1)
         dq2_copy(h).wait_recv()
         dq = (dq + 0.25 * twice(twice(wide(dq2i[h]), 1), 1)) * SCALE
-        gq_ref[:, cols(h)] = nt(back[...], dq.astype(BF16)).astype(BF16)
+        outs[1, h] = nt(back[...], dq.astype(BF16)).astype(BF16)
+        put(1, h).start()
 
     each_head(level0_back)
 
     def finish(h):
         dkv_copy(h).wait_recv()
-        for n, out in enumerate((gk_ref, gv_ref)):
+        for n in range(2):
             total = (
                 dkv0[h, n] + 0.5 * twice(wide(dkvi[h, n]), 0) + 0.25 * twice(twice(dkv2[h, n], 0), 0)
             )
-            out[:, cols(h)] = nn(back[...], total.astype(BF16)).astype(BF16)
+            outs[2 + n, h] = nn(back[...], total.astype(BF16)).astype(BF16)
+            put(2 + n, h).start()
 
     each_head(finish)
 
     def drain(h):
         for make in (kv_copy, q2_copy, a2_copy, g2_copy, dkv_copy, dq2_copy):
             make(h).wait_send()
+        for n in range(4):
+            put(n, h).wait()
 
     each_head(drain)
     x_copy().wait_send()
+
+
+def write_out(*refs):
+    sources, targets, done = refs[:4], refs[4:8], refs[8]
+    rows = sources[0].shape[0] // PIECES
+    copies = [
+        pltpu.make_async_copy(
+            source.at[pl.ds(n * rows, rows)], target.at[pl.ds(n * rows, rows)], done.at[k, n]
+        )
+        for n in range(PIECES)
+        for k, (source, target) in enumerate(zip(sources, targets))
+    ]
+    for one in copies:
+        one.start()
+    for one in copies:
+        one.wait()
 
 
 def shards(queries, key_states, value_states, out_grad):
@@ -302,6 +342,8 @@
         return pltpu.VMEM(shape, dtype)
 
     scratch = [
+        vmem(4, heads, tokens, DH),
+        *[vmem(heads, tokens, DH)] * 4,
         vmem(tokens, tokens), vmem(tokens, tokens),
         vmem(heads, tokens, DH), vmem(heads, tokens, DH), vmem(heads, tokens, DH),
         vmem(heads, DH, tokens), vmem(heads, DH, tokens), vmem(heads, DH, tokens),
@@ -321,22 +363,33 @@
         vmem(heads, 2, tokens, DH, dtype=F32), vmem(heads, 2, quarter, DH, dtype=F32),
         pltpu.SemaphoreType.DMA((7, heads)),
         pltpu.SemaphoreType.DMA((7, heads)),
+        pltpu.SemaphoreType.DMA((4, heads)),
+        pltpu.SemaphoreType.DMA((4, heads)),
     ]
     flops = 2 * heads * DH * tokens * tokens * 12
-    return pl.pallas_call(
+    kept = pl.pallas_call(
         kernel,
         out_shape=[jax.ShapeDtypeStruct((tokens, width), BF16)] * 4,
-        in_specs=[pl.BlockSpec(memory_space=pltpu.VMEM)] * 4,
-        out_specs=[pl.BlockSpec(memory_space=pltpu.VMEM)] * 4,
+        in_specs=[pl.BlockSpec(memory_space=pltpu.HBM)] * 4,
+        out_specs=[pl.BlockSpec(memory_space=pltpu.HBM)] * 4,
         scratch_shapes=scratch,
         compiler_params=pltpu.CompilerParams(
-            collective_id=0, has_side_effects=True, vmem_limit_bytes=48 * 1024 * 1024
+            collective_id=0, has_side_effects=True, vmem_limit_bytes=VMEM
         ),
         cost_estimate=pl.CostEstimate(
             flops=flops, bytes_accessed=16 * tokens * width, transcendentals=heads * tokens * tokens
         ),
         name="hierarchical_attention",
     )(queries, key_states, value_states, out_grad)
+    return pl.pallas_call(
+        write_out,
+        out_shape=[jax.ShapeDtypeStruct((tokens, width), BF16)] * 4,
+        in_specs=[pl.BlockSpec(memory_space=pltpu.HBM)] * 4,
+        out_specs=[pl.BlockSpec(memory_space=pltpu.HBM)] * 4,
+        scratch_shapes=[pltpu.SemaphoreType.DMA((4, PIECES))],
+        compiler_params=pltpu.CompilerParams(vmem_limit_bytes=VMEM),
+        name="write_out",
+    )(*kept)
 
 
 def solution(mesh):

time: 45.8 us -> 106 us (2.31)
  Pallas kernels: 37.5 us -> 105 us
  local copies, waits for them, and re-layouts: 7.33 us -> 0 us
    pallas_call x0 -> x1, Pallas kernels: none -> 64.8 us  [shards(): pl.pallas_call(write_out, out_shape=[jax.ShapeDtypeStruct((tokens, width)...]
    unnamed x12 -> x0, local copies, waits for them, and re-layouts: 7.33 us -> none
    pallas_call x1, Pallas kernels: 37.5 us -> 40.3 us  [shards(): pl.pallas_call(kernel, out_shape=[jax.ShapeDtypeStruct((tokens, width), B...]
where the time goes in v2:
time: 106 us
  Pallas kernels  105 us (99%)
    pallas_call x1, Pallas kernels, shards(): pl.pallas_call(write_out, out_shape=[jax.ShapeDtypeStruct((tokens, width)...  64.8 us
    pallas_call x1, Pallas kernels, shards(): pl.pallas_call(kernel, out_shape=[jax.ShapeDtypeStruct((tokens, width), B...  40.3 us

profile of v2, /device:TPU:0, one launch (start us, length us, event | category | flops | bytes accessed | tf_op | source)
XLA Modules:
  0.0 105.7 jit_solution(1141131589762223411)
XLA Ops:
  0.6 40.3 %hierarchical_attention.1 = (bf16[512,512]{1,0:T(8,128)(2,1)}, bf16[512,512]{1,0:T(8,128)(2,1)}, bf16[512,512]{1,0:T(8,128)(2,1)}, bf16[512,512]{1,0:T(8,128)(2,1)}) custom-call(bf16[512,512]{1,0:T(8,128)(2,1)} %q_ref.1, bf16[512,512]{1,0:T(8,128)(2,1)} %k_ref.1, bf16[512,512]{1,0:T(8,128)(2,1)} %v_ref.1, bf16[512,512]{1,0:T(8,128)(2,1)} %g_ref.1), custom_call_target="tpu_custom_call" | custom-call | flops 3221225472 | bytes 4194304 | tf_op jit(solution)/shard_map/hierarchical_attention/pallas_call | solution.py:370
  40.9 64.8 %write_out.1 = (bf16[512,512]{1,0:T(8,128)(2,1)}, bf16[512,512]{1,0:T(8,128)(2,1)}, bf16[512,512]{1,0:T(8,128)(2,1)}, bf16[512,512]{1,0:T(8,128)(2,1)}) custom-call(bf16[512,512]{1,0:T(8,128)(2,1)} %get-tuple-element.8.refs_0_, bf16[512,512]{1,0:T(8,128)(2,1)} %get-tuple-element.9.refs_1_, bf16[512,512]{1,0:T(8,128)(2,1)} %get-tuple-element.10.refs_2_, ...), custom_call_target="tpu_custom_call" | custom-call | tf_op jit(solution)/shard_map/write_out/pallas_call | solution.py:384

commit v3 on v2

--- a/solution.py
+++ b/solution.py
@@ -16,7 +16,7 @@
 F32 = jnp.float32
 BF16 = jnp.bfloat16
 PIECES = 4
-VMEM = 60 * 1024 * 1024
+VMEM = 103 * 512 * 1024
 PACK = DH + 16
 
 
@@ -58,11 +58,10 @@
 def kernel(
     q_ref, k_ref, v_ref, g_ref,
     no_ref, gq_ref, gk_ref, gv_ref,
-    outs,
     inq, ink, inv, ing, perm, back, qs, ks, vs, kts, vts, dos, p0, p1, p2, a0, a1, rows, att,
     q1, kv1, kv1p, k2c, v2c, q2, q2v, a2o, a2i, xo, xi,
-    g0, g1, g2o, g2i, dq1, dq2o, dq2i, dkvo, dkvi, dkv0, dkv2,
-    send, recv, arrived, written,
+    g0, g1, g2o, g2i, dq0, dq1, dq2o, dq2i, dkvo, dkvi, dkv0, dkv2,
+    send, recv, arrived,
 ):
     tokens, width = q_ref.shape
     heads = width // DH
@@ -101,20 +100,15 @@
         return copy(6, 0, xo, xi, at_core)
 
     def cols(h):
-        return pl.ds(pl.multiple_of(h * DH, DH), DH)
+        return pl.ds(h * DH, DH)
 
     def each_head(body):
-        @pl.loop(0, heads)
-        def _(h):
+        for h in range(heads):
             body(h)
 
     def fetch(n, h):
         source, target = ((k_ref, ink), (v_ref, inv), (q_ref, inq), (g_ref, ing))[n]
         return pltpu.make_async_copy(source.at[:, cols(h)], target.at[h], arrived.at[n, h])
-
-    def put(n, h):
-        target = (no_ref, gq_ref, gk_ref, gv_ref)[n]
-        return pltpu.make_async_copy(outs.at[n, h], target.at[:, cols(h)], written.at[n, h])
 
     barrier = pltpu.get_barrier_semaphore()
     for where in (at_x, at_y, at_core):
@@ -169,9 +163,9 @@
         a0[h] = nn(vt, p)
         rows[h, 0:1, :] = m
         rows[h, 1:2, :] = s
-        fetch(3, h).wait()
         dos[h] = nn(perm[...], ing[h]).T.astype(BF16)
 
+    each_head(lambda h: fetch(3, h).wait())
     each_head(level0)
     back[...] = jnp.where(order(minor) == major, 1.0, 0.0).astype(BF16)
 
@@ -230,8 +224,7 @@
     xo[...] = jnp.zeros_like(xo)
     coarse(0)
 
-    @pl.loop(1, heads)
-    def _(h):
+    for h in range(1, heads):
         coarse(h)
         combine(h - 1)
 
@@ -283,35 +276,35 @@
     each_head(coarse_back)
 
     def level0_back(h):
-        outs[0, h] = nt(back[...], (wide(att[h]) * inverse).astype(BF16)).astype(BF16)
-        put(0, h).start()
+        no_ref[:, cols(h)] = nt(back[...], (wide(att[h]) * inverse).astype(BF16)).astype(BF16)
         ds = score_grads(p0[h], vs[h], g0[h], rows[h, 5:6, :])
         dkv0[h, 0] = nn(ds, qs[h]) * SCALE
         dkv0[h, 1] = nt(p0[h], g0[h])
-        dq = nn(kts[h], ds) + 0.5 * twice(dq1[h], 1)
-        dq2_copy(h).wait_recv()
+        dq0[h] = nn(kts[h], ds) + 0.5 * twice(dq1[h], 1)
+
+    each_head(level0_back)
+    each_head(lambda h: dq2_copy(h).wait_recv())
+
+    def finish_q(h):
+        dq = dq0[h]
         dq = (dq + 0.25 * twice(twice(wide(dq2i[h]), 1), 1)) * SCALE
-        outs[1, h] = nt(back[...], dq.astype(BF16)).astype(BF16)
-        put(1, h).start()
-
-    each_head(level0_back)
+        gq_ref[:, cols(h)] = nt(back[...], dq.astype(BF16)).astype(BF16)
+
+    each_head(finish_q)
 
     def finish(h):
         dkv_copy(h).wait_recv()
-        for n in range(2):
+        for n, out in enumerate((gk_ref, gv_ref)):
             total = (
                 dkv0[h, n] + 0.5 * twice(wide(dkvi[h, n]), 0) + 0.25 * twice(twice(dkv2[h, n], 0), 0)
             )
-            outs[2 + n, h] = nn(back[...], total.astype(BF16)).astype(BF16)
-            put(2 + n, h).start()
+            out[:, cols(h)] = nn(back[...], total.astype(BF16)).astype(BF16)
 
     each_head(finish)
 
     def drain(h):
         for make in (kv_copy, q2_copy, a2_copy, g2_copy, dkv_copy, dq2_copy):
             make(h).wait_send()
-        for n in range(4):
-            put(n, h).wait()
 
     each_head(drain)
     x_copy().wait_send()
@@ -342,7 +335,6 @@
         return pltpu.VMEM(shape, dtype)
 
     scratch = [
-        vmem(4, heads, tokens, DH),
         *[vmem(heads, tokens, DH)] * 4,
         vmem(tokens, tokens), vmem(tokens, tokens),
         vmem(heads, tokens, DH), vmem(heads, tokens, DH), vmem(heads, tokens, DH),
@@ -357,13 +349,12 @@
         vmem(8, tokens, dtype=F32), vmem(8, tokens, dtype=F32),
         vmem(heads, DH, tokens), vmem(heads, DH, half),
         vmem(heads, PACK, quarter), vmem(heads, PACK, quarter),
-        vmem(heads, DH, half, dtype=F32),
+        vmem(heads, DH, tokens, dtype=F32), vmem(heads, DH, half, dtype=F32),
         vmem(heads, DH, quarter), vmem(heads, DH, quarter),
         vmem(heads, 2, half, DH), vmem(heads, 2, half, DH),
         vmem(heads, 2, tokens, DH, dtype=F32), vmem(heads, 2, quarter, DH, dtype=F32),
         pltpu.SemaphoreType.DMA((7, heads)),
         pltpu.SemaphoreType.DMA((7, heads)),
-        pltpu.SemaphoreType.DMA((4, heads)),
         pltpu.SemaphoreType.DMA((4, heads)),
     ]
     flops = 2 * heads * DH * tokens * tokens * 12
@@ -371,7 +362,7 @@
         kernel,
         out_shape=[jax.ShapeDtypeStruct((tokens, width), BF16)] * 4,
         in_specs=[pl.BlockSpec(memory_space=pltpu.HBM)] * 4,
-        out_specs=[pl.BlockSpec(memory_space=pltpu.HBM)] * 4,
+        out_specs=[pl.BlockSpec(memory_space=pltpu.VMEM)] * 4,
         scratch_shapes=scratch,
         compiler_params=pltpu.CompilerParams(
             collective_id=0, has_side_effects=True, vmem_limit_bytes=VMEM
@@ -384,7 +375,7 @@
     return pl.pallas_call(
         write_out,
         out_shape=[jax.ShapeDtypeStruct((tokens, width), BF16)] * 4,
-        in_specs=[pl.BlockSpec(memory_space=pltpu.HBM)] * 4,
+        in_specs=[pl.BlockSpec(memory_space=pltpu.VMEM)] * 4,
         out_specs=[pl.BlockSpec(memory_space=pltpu.HBM)] * 4,
         scratch_shapes=[pltpu.SemaphoreType.DMA((4, PIECES))],
         compiler_params=pltpu.CompilerParams(vmem_limit_bytes=VMEM),

time: 106 us -> 40.6 us (0.38)
  Pallas kernels: 105 us -> 39.6 us
    pallas_call x1, Pallas kernels: 64.8 us -> 1.44 us  [shards(): pl.pallas_call(write_out, out_shape=[jax.ShapeDtypeStruct((tokens, width)...]
    pallas_call x1, Pallas kernels: 40.3 us -> 38.2 us  [shards(): pl.pallas_call(kernel, out_shape=[jax.ShapeDtypeStruct((tokens, width), B...]
where the time goes in v3:
time: 40.6 us; the launch traced here: 40.4 us
  Pallas kernels  39.6 us (98%)
  between operations  0.8 us (2%)
    pallas_call x1, Pallas kernels, shards(): pl.pallas_call(kernel, out_shape=[jax.ShapeDtypeStruct((tokens, width), B...  38.2 us
    pallas_call x1, Pallas kernels, shards(): pl.pallas_call(write_out, out_shape=[jax.ShapeDtypeStruct((tokens, width)...  1.44 us

profile of v3, /device:TPU:0, one launch (start us, length us, event | category | flops | bytes accessed | tf_op | source)
XLA Modules:
  0.0 40.4 jit_solution(16589731605144991156)
XLA Ops:
  0.6 38.2 %hierarchical_attention.1 = (bf16[512,512]{1,0:T(8,128)(2,1)S(1)}, bf16[512,512]{1,0:T(8,128)(2,1)S(1)}, bf16[512,512]{1,0:T(8,128)(2,1)S(1)}, bf16[512,512]{1,0:T(8,128)(2,1)S(1)}) custom-call(bf16[512,512]{1,0:T(8,128)(2,1)} %q_ref.1, bf16[512,512]{1,0:T(8,128)(2,1)} %k_ref.1, bf16[512,512]{1,0:T(8,128)(2,1)} %v_ref.1, bf16[512,512]{1,0:T(8,128)(2,1)} %g_ref.1), custom_call_target="tpu_custom_call" | custom-call | flops 3221225472 | bytes 4194304 | tf_op jit(solution)/shard_map/hierarchical_attention/pallas_call | solution.py:361
  38.8 1.4 %write_out.1 = (bf16[512,512]{1,0:T(8,128)(2,1)}, bf16[512,512]{1,0:T(8,128)(2,1)}, bf16[512,512]{1,0:T(8,128)(2,1)}, bf16[512,512]{1,0:T(8,128)(2,1)}) custom-call(bf16[512,512]{1,0:T(8,128)(2,1)S(1)} %get-tuple-element.8.refs_0_, bf16[512,512]{1,0:T(8,128)(2,1)S(1)} %get-tuple-element.9.refs_1_, bf16[512,512]{1,0:T(8,128)(2,1)S(1)} %get-tuple-element.10.refs_2_, ...), custom_call_target="tpu_custom_call" | custom-call | tf_op jit(solution)/shard_map/write_out/pallas_call | solution.py:375

commit v4 on v3

--- a/solution.py
+++ b/solution.py
@@ -60,7 +60,7 @@
     no_ref, gq_ref, gk_ref, gv_ref,
     inq, ink, inv, ing, perm, back, qs, ks, vs, kts, vts, dos, p0, p1, p2, a0, a1, rows, att,
     q1, kv1, kv1p, k2c, v2c, q2, q2v, a2o, a2i, xo, xi,
-    g0, g1, g2o, g2i, dq0, dq1, dq2o, dq2i, dkvo, dkvi, dkv0, dkv2,
+    g0, g1, g2o, g2i, dq0, dq1, dq2o, dq2i, dkvo, dkvi, dkv0, dkv1, dkv2,
     send, recv, arrived,
 ):
     tokens, width = q_ref.shape
@@ -119,14 +119,13 @@
             for n in group:
                 fetch(n, h).start()
 
-    def order(p):
-        slab = p // quarter
-        return 4 * (p % quarter) + slab // 2 + 2 * (slab % 2)
-
-    shape = (tokens, tokens)
-    major = lax.broadcasted_iota(jnp.int32, shape, 0)
-    minor = lax.broadcasted_iota(jnp.int32, shape, 1)
-    perm[...] = jnp.where(order(major) == minor, 1.0, 0.0).astype(BF16)
+    bits = quarter.bit_length() - 1
+    lane = lax.broadcasted_iota(jnp.int32, (1, tokens), 1)
+    slab = lane >> bits
+    token_of = ((lane & (quarter - 1)) << 2) + (slab >> 1) + ((slab & 1) << 1)
+    place_of = (lane >> 2) + (((lane >> 1) & 1) << bits) + ((lane & 1) << (bits + 1))
+    major = lax.broadcasted_iota(jnp.int32, (tokens, tokens), 0)
+    perm[...] = jnp.where(place_of == major, 1.0, 0.0).astype(BF16)
     pl.semaphore_wait(barrier, 3)
 
     def load_kv(h):
@@ -167,7 +166,7 @@
 
     each_head(lambda h: fetch(3, h).wait())
     each_head(level0)
-    back[...] = jnp.where(order(minor) == major, 1.0, 0.0).astype(BF16)
+    back[...] = jnp.where(token_of == major, 1.0, 0.0).astype(BF16)
 
     def coarse(h):
         kv_copy(h).wait_recv()
@@ -248,17 +247,17 @@
         rows[h, 5:6, :] = w0 * along
         rows[h, 6:7, :] = twice(fold(w1 * along), 1)
 
-    each_head(cotangents)
-
     def score_grads(p, values, grads, delta):
         return (wide(p) * (nn(values, grads) - delta)).astype(BF16)
 
-    def coarse_back(h):
+    def level1_back(h):
         k1p, v1p = kv1p[h, 0], kv1p[h, 1]
         ds = score_grads(p1[h], v1p, g1[h], rows[h, 6:7, 0:half])
-        dk = nn(ds, q1[h])
-        dv = nt(p1[h], g1[h])
+        dkv1[0] = nn(ds, q1[h])
+        dkv1[1] = nt(p1[h], g1[h])
         dq1[h] = nn(flip(k1p), ds)
+
+    def level2_back(h):
         g2_copy(h).wait_recv()
         figures = wide(g2i[h, DH:PACK])
         grads = g2i[h, 0:DH]
@@ -267,13 +266,21 @@
         dv2 = nt(p2[h], grads)
         dq2o[h] = nn(flip(k2c[h]), ds).astype(BF16)
         dq2_copy(h).start()
-        dkvo[h, 0] = ((dk + 0.5 * twice(dk2[quarter:], 0)) * SCALE).astype(BF16)
-        dkvo[h, 1] = (dv + 0.5 * twice(dv2[quarter:], 0)).astype(BF16)
+        dkvo[h, 0] = ((dkv1[0] + 0.5 * twice(dk2[quarter:], 0)) * SCALE).astype(BF16)
+        dkvo[h, 1] = (dkv1[1] + 0.5 * twice(dv2[quarter:], 0)).astype(BF16)
         dkv_copy(h).start()
         dkv2[h, 0] = dk2[:quarter] * SCALE
         dkv2[h, 1] = dv2[:quarter]
 
-    each_head(coarse_back)
+    cotangents(0)
+    cotangents(1)
+    level1_back(0)
+    for h in range(2, heads):
+        cotangents(h)
+    level2_back(0)
+    for h in range(1, heads):
+        level1_back(h)
+        level2_back(h)
 
     def level0_back(h):
         no_ref[:, cols(h)] = nt(back[...], (wide(att[h]) * inverse).astype(BF16)).astype(BF16)
@@ -352,7 +359,8 @@
         vmem(heads, DH, tokens, dtype=F32), vmem(heads, DH, half, dtype=F32),
         vmem(heads, DH, quarter), vmem(heads, DH, quarter),
         vmem(heads, 2, half, DH), vmem(heads, 2, half, DH),
-        vmem(heads, 2, tokens, DH, dtype=F32), vmem(heads, 2, quarter, DH, dtype=F32),
+        vmem(heads, 2, tokens, DH, dtype=F32), vmem(2, half, DH, dtype=F32),
+        vmem(heads, 2, quarter, DH, dtype=F32),
         pltpu.SemaphoreType.DMA((7, heads)),
         pltpu.SemaphoreType.DMA((7, heads)),
         pltpu.SemaphoreType.DMA((4, heads)),

time: 40.6 us -> 40.5 us (level)
  no operation moved by 1% of the time
where the time goes in v4:
time: 40.5 us; the launch traced here: 40.3 us
  Pallas kernels  39.5 us (98%)
  between operations  0.8 us (2%)
    pallas_call x1, Pallas kernels, shards(): pl.pallas_call(kernel, out_shape=[jax.ShapeDtypeStruct((tokens, width), B...  38.1 us
    pallas_call x1, Pallas kernels, shards(): pl.pallas_call(write_out, out_shape=[jax.ShapeDtypeStruct((tokens, width)...  1.44 us

profile of v4, /device:TPU:0, one launch (start us, length us, event | category | flops | bytes accessed | tf_op | source)
XLA Modules:
  0.0 40.3 jit_solution(16779077933620204837)
XLA Ops:
  0.6 38.1 %hierarchical_attention.1 = (bf16[512,512]{1,0:T(8,128)(2,1)S(1)}, bf16[512,512]{1,0:T(8,128)(2,1)S(1)}, bf16[512,512]{1,0:T(8,128)(2,1)S(1)}, bf16[512,512]{1,0:T(8,128)(2,1)S(1)}) custom-call(bf16[512,512]{1,0:T(8,128)(2,1)} %q_ref.1, bf16[512,512]{1,0:T(8,128)(2,1)} %k_ref.1, bf16[512,512]{1,0:T(8,128)(2,1)} %v_ref.1, bf16[512,512]{1,0:T(8,128)(2,1)} %g_ref.1), custom_call_target="tpu_custom_call" | custom-call | flops 3221225472 | bytes 4194304 | tf_op jit(solution)/shard_map/hierarchical_attention/pallas_call | solution.py:369
  38.7 1.4 %write_out.1 = (bf16[512,512]{1,0:T(8,128)(2,1)}, bf16[512,512]{1,0:T(8,128)(2,1)}, bf16[512,512]{1,0:T(8,128)(2,1)}, bf16[512,512]{1,0:T(8,128)(2,1)}) custom-call(bf16[512,512]{1,0:T(8,128)(2,1)S(1)} %get-tuple-element.8.refs_0_, bf16[512,512]{1,0:T(8,128)(2,1)S(1)} %get-tuple-element.9.refs_1_, bf16[512,512]{1,0:T(8,128)(2,1)S(1)} %get-tuple-element.10.refs_2_, ...), custom_call_target="tpu_custom_call" | custom-call | tf_op jit(solution)/shard_map/write_out/pallas_call | solution.py:383

commit v5 on v4

--- a/solution.py
+++ b/solution.py
@@ -58,7 +58,7 @@
 def kernel(
     q_ref, k_ref, v_ref, g_ref,
     no_ref, gq_ref, gk_ref, gv_ref,
-    inq, ink, inv, ing, perm, back, qs, ks, vs, kts, vts, dos, p0, p1, p2, a0, a1, rows, att,
+    inkv, inqg, perm, back, qs, ks, vs, kts, vts, dos, p0, p1, p2, a0, a1, rows, att,
     q1, kv1, kv1p, k2c, v2c, q2, q2v, a2o, a2i, xo, xi,
     g0, g1, g2o, g2i, dq0, dq1, dq2o, dq2i, dkvo, dkvi, dkv0, dkv1, dkv2,
     send, recv, arrived,
@@ -107,17 +107,18 @@
             body(h)
 
     def fetch(n, h):
-        source, target = ((k_ref, ink), (v_ref, inv), (q_ref, inq), (g_ref, ing))[n]
-        return pltpu.make_async_copy(source.at[:, cols(h)], target.at[h], arrived.at[n, h])
+        source, target = ((k_ref, inkv), (v_ref, inkv), (q_ref, inqg), (g_ref, inqg))[n]
+        return pltpu.make_async_copy(
+            source.at[:, cols(h)], target.at[h, :, cols(n % 2)], arrived.at[n, h]
+        )
 
     barrier = pltpu.get_barrier_semaphore()
     for where in (at_x, at_y, at_core):
         pl.semaphore_signal(barrier, inc=1, device_id=where, device_id_type=MESH)
 
-    for group in ((0, 1), (2, 3)):
-        for h in range(heads):
-            for n in group:
-                fetch(n, h).start()
+    for h in range(heads):
+        for n in range(4):
+            fetch(n, h).start()
 
     bits = quarter.bit_length() - 1
     lane = lax.broadcasted_iota(jnp.int32, (1, tokens), 1)
@@ -128,26 +129,25 @@
     perm[...] = jnp.where(place_of == major, 1.0, 0.0).astype(BF16)
     pl.semaphore_wait(barrier, 3)
 
-    def load_kv(h):
-        for n, (ref, kept) in enumerate(((ink, ks), (inv, vs))):
-            fetch(n, h).wait()
-            moved = nn(perm[...], ref[h])
-            kept[h] = moved.astype(BF16)
-            kv1[h, n] = halve(moved)
+    def load(h):
+        fetch(0, h).wait()
+        fetch(1, h).wait()
+        moved = nn(perm[...], inkv[h])
+        for n, kept in enumerate((ks, vs)):
+            kept[h] = moved[:, n * DH : (n + 1) * DH].astype(BF16)
+            kv1[h, n] = halve(moved[:, n * DH : (n + 1) * DH])
         kv_copy(h).start()
-
-    each_head(load_kv)
-
-    def load_q(h):
         fetch(2, h).wait()
-        moved = nn(perm[...], inq[h])
-        qs[h] = moved.astype(BF16)
-        first = halve(moved)
+        fetch(3, h).wait()
+        moved = nn(perm[...], inqg[h])
+        qs[h] = moved[:, :DH].astype(BF16)
+        first = halve(moved[:, :DH])
         q1[h] = first
         q2[h] = halve(first)
         q2_copy(h).start()
-
-    each_head(load_q)
+        dos[h] = moved[:, DH:].T.astype(BF16)
+
+    each_head(load)
 
     def softmax(scores):
         top = jnp.max(scores, axis=0, keepdims=True)
@@ -162,9 +162,7 @@
         a0[h] = nn(vt, p)
         rows[h, 0:1, :] = m
         rows[h, 1:2, :] = s
-        dos[h] = nn(perm[...], ing[h]).T.astype(BF16)
-
-    each_head(lambda h: fetch(3, h).wait())
+
     each_head(level0)
     back[...] = jnp.where(token_of == major, 1.0, 0.0).astype(BF16)
 
@@ -283,7 +281,6 @@
         level2_back(h)
 
     def level0_back(h):
-        no_ref[:, cols(h)] = nt(back[...], (wide(att[h]) * inverse).astype(BF16)).astype(BF16)
         ds = score_grads(p0[h], vs[h], g0[h], rows[h, 5:6, :])
         dkv0[h, 0] = nn(ds, qs[h]) * SCALE
         dkv0[h, 1] = nt(p0[h], g0[h])
@@ -295,17 +292,25 @@
     def finish_q(h):
         dq = dq0[h]
         dq = (dq + 0.25 * twice(twice(wide(dq2i[h]), 1), 1)) * SCALE
-        gq_ref[:, cols(h)] = nt(back[...], dq.astype(BF16)).astype(BF16)
+        pair = jnp.concatenate([(wide(att[h]) * inverse).astype(BF16), dq.astype(BF16)], 0)
+        ordered = nt(back[...], pair).astype(BF16)
+        no_ref[:, cols(h)] = ordered[:, :DH]
+        gq_ref[:, cols(h)] = ordered[:, DH:]
 
     each_head(finish_q)
 
     def finish(h):
         dkv_copy(h).wait_recv()
-        for n, out in enumerate((gk_ref, gv_ref)):
-            total = (
+        pair = jnp.concatenate(
+            [
                 dkv0[h, n] + 0.5 * twice(wide(dkvi[h, n]), 0) + 0.25 * twice(twice(dkv2[h, n], 0), 0)
-            )
-            out[:, cols(h)] = nn(back[...], total.astype(BF16)).astype(BF16)
+                for n in range(2)
+            ],
+            1,
+        )
+        ordered = nn(back[...], pair.astype(BF16)).astype(BF16)
+        gk_ref[:, cols(h)] = ordered[:, :DH]
+        gv_ref[:, cols(h)] = ordered[:, DH:]
 
     each_head(finish)
 
@@ -342,7 +347,7 @@
         return pltpu.VMEM(shape, dtype)
 
     scratch = [
-        *[vmem(heads, tokens, DH)] * 4,
+        vmem(heads, tokens, 2 * DH), vmem(heads, tokens, 2 * DH),
         vmem(tokens, tokens), vmem(tokens, tokens),
         vmem(heads, tokens, DH), vmem(heads, tokens, DH), vmem(heads, tokens, DH),
         vmem(heads, DH, tokens), vmem(heads, DH, tokens), vmem(heads, DH, tokens),

time: 40.5 us -> 39.9 us (0.985)
    pallas_call x1, Pallas kernels: 38.1 us -> 37.7 us  [shards(): pl.pallas_call(kernel, out_shape=[jax.ShapeDtypeStruct((tokens, width), B...]
where the time goes in v5:
time: 39.9 us; the launch traced here: 39.7 us
  Pallas kernels  39.1 us (98%)
  between operations  0.64 us (2%)
    pallas_call x1, Pallas kernels, shards(): pl.pallas_call(kernel, out_shape=[jax.ShapeDtypeStruct((tokens, width), B...  37.7 us
    pallas_call x1, Pallas kernels, shards(): pl.pallas_call(write_out, out_shape=[jax.ShapeDtypeStruct((tokens, width)...  1.44 us

profile of v5, /device:TPU:0, one launch (start us, length us, event | category | flops | bytes accessed | tf_op | source)
XLA Modules:
  0.0 39.7 jit_solution(17840816450351288071)
XLA Ops:
  0.6 37.7 %hierarchical_attention.1 = (bf16[512,512]{1,0:T(8,128)(2,1)S(1)}, bf16[512,512]{1,0:T(8,128)(2,1)S(1)}, bf16[512,512]{1,0:T(8,128)(2,1)S(1)}, bf16[512,512]{1,0:T(8,128)(2,1)S(1)}) custom-call(bf16[512,512]{1,0:T(8,128)(2,1)} %q_ref.1, bf16[512,512]{1,0:T(8,128)(2,1)} %k_ref.1, bf16[512,512]{1,0:T(8,128)(2,1)} %v_ref.1, bf16[512,512]{1,0:T(8,128)(2,1)} %g_ref.1), custom_call_target="tpu_custom_call" | custom-call | flops 3221225472 | bytes 4194304 | tf_op jit(solution)/shard_map/hierarchical_attention/pallas_call | solution.py:374
  38.3 1.4 %write_out.1 = (bf16[512,512]{1,0:T(8,128)(2,1)}, bf16[512,512]{1,0:T(8,128)(2,1)}, bf16[512,512]{1,0:T(8,128)(2,1)}, bf16[512,512]{1,0:T(8,128)(2,1)}) custom-call(bf16[512,512]{1,0:T(8,128)(2,1)S(1)} %get-tuple-element.8.refs_0_, bf16[512,512]{1,0:T(8,128)(2,1)S(1)} %get-tuple-element.9.refs_1_, bf16[512,512]{1,0:T(8,128)(2,1)S(1)} %get-tuple-element.10.refs_2_, ...), custom_call_target="tpu_custom_call" | custom-call | tf_op jit(solution)/shard_map/write_out/pallas_call | solution.py:388
